TPU v7x, 128 devices: a whole 4x4x4 slice. The times are simulated.
128 devices in a mesh: ckpt: 8 (over y_hi, x), row: 16 (over y_lo, z, core).
Axes of the slice: x: 4, y: 4 (y_hi: 2, y_lo: 2; y = y_hi * 2 + y_lo), z: 4, core: 2. Of those that a mesh axis runs over, the one named last changes fastest.
Arguments:
- quant_codes: bfloat16 [8, 16384, 8192], P('ckpt', 'row'), may hold values from -127 to 127, as said below
- exponents: int32 [8, 128, 64], P('ckpt', 'row'), may hold values from -8 to -4
- numerators: int32 [8], replicated, may hold values from 1 to 9
- denominator: int32 [1], replicated, may hold values from 16 to 64
Outputs:
- block_tiles: bfloat16 [16384, 8192], P('ckpt', 'row')
- block_scales: float32 [128, 64], P('ckpt', 'row')
Inputs may be any that keep to these rules, and one draw needn't show every extreme that they name: `quant_codes`: every entry is a whole number.
All inputs are finite; a program needn't handle non-finite values. Where the computation divides by a largest or mean magnitude, that divisor is 1e-20 or more.
Results may differ from a plain program's by a relative error of at most 0.001.
Values may be sent and summed in bfloat16 or wider, within the bound.
No kernel may reach another device: no remote copies, remote signals or barrier semaphores. Data moves between devices by JAX's collectives and lax.ppermute only.
A program may use at most 256 MiB of HBM per device.

v0:
```python
import jax
import jax.numpy as jnp
from jax import lax
from jax.sharding import PartitionSpec as P

BLOCK = 128


epsilon = 1e-06


def weigh_codes(slab_codes, powers_block, own_weights):
    ckpt_count, row_count, col_count = slab_codes.shape
    grid_values = slab_codes.astype(jnp.float32).reshape(
        ckpt_count, row_count // BLOCK, BLOCK, col_count // BLOCK, BLOCK
    )
    scaled = grid_values * powers_block[:, :, None, :, None]
    weighted = jnp.sum(own_weights[:, None, None, None, None] * scaled, axis=0)
    return weighted.reshape(row_count, col_count)


def body(quant_codes, exponents, numerators, denominator):
    ckpt_count = quant_codes.shape[0]
    first_index = lax.axis_index("ckpt") * ckpt_count
    own_weights = lax.dynamic_slice_in_dim(numerators, first_index, ckpt_count, 0).astype(
        jnp.float32
    )
    powers_all = jnp.exp2(exponents.astype(jnp.float32))
    partial_rows = weigh_codes(quant_codes, powers_all, own_weights)
    relaid = lax.all_to_all(partial_rows, "row", split_axis=1, concat_axis=0, tiled=True)
    summed = lax.psum_scatter(relaid, "ckpt", scatter_dimension=0, tiled=True)
    average = summed / denominator[0].astype(jnp.float32)
    row_count, col_count = average.shape
    grid_average = average.reshape(row_count // BLOCK, BLOCK, col_count // BLOCK, BLOCK)
    block_scales = jnp.max(jnp.abs(grid_average), axis=(1, 3))
    block_tiles = grid_average / (block_scales + epsilon)[:, None, :, None]
    return (block_tiles.reshape(row_count, col_count).astype(jnp.bfloat16), block_scales)


def solution(mesh):
    placed = (P("ckpt", "row", None), P("ckpt", "row", None), P(), P())
    return jax.shard_map(
        body,
        mesh=mesh,
        in_specs=placed,
        out_specs=(P("ckpt", "row"), P("ckpt", "row")),
        check_vma=False,
    )
```

profile of v0, /device:TPU:0, one launch (start us, length us, event | category | flops | bytes accessed | tf_op | source)
XLA Modules:
  0.0 894.1 jit_solution(13908843566437502486)
XLA Ops:
  7.2 0.0 reduce-scatter.2.cloned.1.call-start
  7.2 1.2 dynamic_slice.3
  9.1 0.7 exponential_bitcast_fusion
  9.8 11.3 %mul.33 = f32[8,128,64,128]{3,2,1,0:T(8,128)} broadcast(f32[8,64]{1,0:T(8,128)S(1)} %exponential_bitcast_fusion), dimensions={0,2} | broadcast | bytes 33556480 | tf_op jit(solution)/shard_map/mul | solution.py:17
  21.1 35.8 %mul.34 = f32[1024,16,512]{2,1,0:T(8,128)} reshape(f32[8,128,64,128]{3,2,1,0:T(8,128)} %mul.33) | data formatting | bytes 67108864 | tf_op jit(solution)/shard_map/mul | solution.py:17
  56.9 19.6 %copy.13 = f32[128,8,16,512]{3,2,1,0:T(8,128)} copy(bf16[128,8,16,512]{3,1,2,0:T(8,128)(2,1)} %bitcast.23) | data formatting | bytes 50331648
  76.5 33.6 %fusion = f32[1024,16,512]{2,1,0:T(8,128)} fusion(f32[1024,16,512]{2,1,0:T(8,128)} %mul.34, f32[128,8,16,512]{3,2,1,0:T(8,128)} %copy.13, f32[]{:T(128)} %bitcast), kind=kLoop, calls=%fused_computation.1 | loop fusion | flops 16777216 | bytes 100663296 | tf_op jit(solution)/shard_map/mul | solution.py:18
  110.1 28.2 %copy.11 = f32[1024,16,512]{2,0,1:T(8,128)S(1)} copy(f32[1024,16,512]{2,1,0:T(8,128)} %fusion) | data formatting | bytes 67108864 | tf_op jit(solution)/shard_map/mul | solution.py:18
  138.3 372.3 %all_to_all.16 = f32[1024,16,512]{2,0,1:T(8,128)} all-to-all(f32[1024,16,512]{2,0,1:T(8,128)S(1)} %copy.11), channel_id=1, replica_groups=mesh['ckpt'=8,'row'=16] {'row'}, dimensions={1} | all-to-all | bytes 67108864 | tf_op jit(solution)/shard_map/all_to_all | solution.py:30
  510.6 0.0 reduce-scatter.2.cloned.1.call-update
  511.3 358.1 %reduce-scatter.2.cloned.1.call-done = f32[2048,512]{1,0:T(8,128)} async-done(((f32[16384,512]{1,0:T(8,128)}), f32[2048,512]{1,0:T(8,128)}) %reduce-scatter.2.cloned.1.call-update) | async-done | bytes 4194320 | tf_op jit(solution)/shard_map/reduce_scatter | solution.py:31
  869.4 4.6 divide_abs_fusion
  874.0 5.2 abs.7
  879.3 2.9 reduce_max.9
  882.1 0.7 copy.12
  882.8 0.0 copy-start
  882.8 0.6 div.20
  883.4 1.6 copy-done
  885.0 2.2 fusion.1
  (1 shorter events, 0.0 us)
Async XLA Ops:
  7.2 862.2 %reduce-scatter.2.cloned.1.call-start = ((), (), s32[]{:S(2)}) async-start(), calls=%async_computation.2 | async-start | bytes 37748736 | tf_op jit(solution)/shard_map/reduce_scatter | solution.py:31
  882.8 2.2 copy-start
Sparse Core Ops, SparseCore 0:
  510.8 358.5 reduce-scatter.1
where the time goes:
time: 896 us; the launch traced here: 894 us
  blocking collectives  372 us (42%)
  waiting for transfers between devices  358 us (40%)
  local copies, waits for them, and re-layouts  104 us (12%)
  other arithmetic  44.1 us (5%)
  between operations  15.4 us (2%)
    all_to_all x1, blocking collectives, body(): lax.all_to_all(partial_rows, 'row', split_axis=1, concat_axis=0, tiled=True)  372 us
    reduce_scatter x1, waiting for transfers between devices, body(): summed = lax.psum_scatter(relaid, 'ckpt', scatter_dimension=0, tiled=True)  358 us
    mul x2, local copies, waits for them, and re-layouts, weigh_codes(): scaled = grid_values * powers_block[:, :, None, :, None]  47.1 us
    mul x1, other arithmetic, weigh_codes(): weighted = jnp.sum(own_weights[:, None, None, None, None] * scaled, axis=0)  33.6 us
    mul x1, local copies, waits for them, and re-layouts, weigh_codes(): weighted = jnp.sum(own_weights[:, None, None, None, None] * scaled, axis=0)  28.2 us
    unnamed x4, local copies, waits for them, and re-layouts  21.8 us
  transfers between devices with their start and end apart: 1, of which 1 were waited for; matrix products, arithmetic and copies ran while one was open for 0% of the time, Pallas kernels for 0%

commit v1 on v0

v1 whole, which is shorter than its diff:
```python
import jax
import jax.numpy as jnp
from jax import lax
from jax.experimental import pallas as pl
from jax.experimental.pallas import tpu as pltpu
from jax.sharding import PartitionSpec as P

BLOCK = 128
EPSILON = 1e-6
AXES = ("ckpt", "row")
OWN, PARTNER, KEEP, YHI, SHIFT, FLIP = range(6)
TILE_COLS = 512
CHUNK = 256
CHUNKS = 1024 // CHUNK
BANDS = CHUNK // BLOCK
EXTRA = CHUNK // 16
SPAN = TILE_COLS // BLOCK


def device_index(x, y, z, core):
    y_hi, y_lo = divmod(y, 2)
    return (y_hi * 4 + x) * 16 + y_lo * 8 + z * 2 + core


def permutation(target):
    return [
        (device_index(x, y, z, core), device_index(*target(x, y, z, core)))
        for x in range(4)
        for y in range(4)
        for z in range(4)
        for core in range(2)
    ]


def pair_of(x, core):
    return x + 1 - 2 * ((x + core) % 2)


ACROSS = {0: 1, 1: 3, 2: 0, 3: 2}
BESIDE = {0: 0, 1: 2, 2: 1, 3: 3}
PAIR_PERM = permutation(lambda x, y, z, core: (pair_of(x, core) % 4, y, z, core))
ACROSS_PERM = permutation(lambda x, y, z, core: (x, ACROSS[y], z, core))
BESIDE_PERM = permutation(lambda x, y, z, core: (x, BESIDE[y], z, core))
Z_PERMS = [permutation(lambda x, y, z, core, m=m: (x, y, (z - x - m) % 4, core)) for m in range(4)]
X_PERMS = [
    permutation(lambda x, y, z, core, m=m: ((x + z + m) % 4, y, z, core ^ (x % 2))) for m in range(4)
]
ZX_PERMS = [
    permutation(lambda x, y, z, core, m=m: (z, y, (z - x - m) % 4, core ^ (x % 2))) for m in range(4)
]


def call(kernel, grid, scalars, inputs, outputs, after=()):
    held = len(after)

    def whole(*refs):
        kernel(*refs[: len(scalars) + len(inputs)], *refs[len(scalars) + len(inputs) + held :])

    moved = sum(a.dtype.itemsize * a.size for a, _, _ in inputs) + sum(
        jnp.dtype(d).itemsize * s[0] * s[1] for s, d, _, _ in outputs
    )
    return pl.pallas_call(
        whole,
        grid_spec=pltpu.PrefetchScalarGridSpec(
            num_scalar_prefetch=len(scalars),
            grid=grid,
            in_specs=[pl.BlockSpec(b, m) for _, b, m in inputs] + [pl.BlockSpec(memory_space=pl.ANY)] * held,
            out_specs=[pl.BlockSpec(b, m) for _, _, b, m in outputs],
        ),
        out_shape=[jax.ShapeDtypeStruct(s, d) for s, d, _, _ in outputs],
        compiler_params=pltpu.CompilerParams(vmem_limit_bytes=40 * 1024 * 1024),
        cost_estimate=pl.CostEstimate(flops=0, bytes_accessed=moved, transcendentals=0),
    )(*scalars, *[a for a, _, _ in inputs], *after)


def block_of(band, col):
    return pl.ds(band * BLOCK, BLOCK), pl.ds(col * BLOCK, BLOCK)


def pack(chunk, place, codes, after):
    def kernel(place, codes, sent):
        sent[...] = codes[0]

    return call(
        kernel,
        (8,),
        [place],
        [(codes, (1, CHUNK, TILE_COLS), lambda j, place: (0, chunk, 2 * j + 1 - place[KEEP]))],
        [((CHUNK, 8 * TILE_COLS), jnp.bfloat16, (CHUNK, TILE_COLS), lambda j, place: (0, j))],
        after,
    )[0]


def add_pairs(chunk, place, weights, own_exps, partner_exps, codes, received):
    def kernel(place, weights, own_exps, partner_exps, c_far, c_near, r_far, r_near, far, near):
        own_weight, partner_weight = weights[place[OWN]], weights[place[PARTNER]]
        z_to = pl.program_id(0)
        for y_lo, kept, came, out in (
            (1 - place[YHI], c_far, r_far, far),
            (place[YHI], c_near, r_near, near),
        ):
            first = (y_lo * 8 + z_to * 2 + place[KEEP]) * SPAN
            for band in range(BANDS):
                for col in range(SPAN):
                    own = own_exps[chunk * BANDS + band, first + col]
                    partner = partner_exps[chunk * BANDS + band, first + col]
                    unit = jnp.minimum(own, partner)
                    own_scale = (own_weight << (own - unit)).astype(jnp.float32)
                    partner_scale = (partner_weight << (partner - unit)).astype(jnp.float32)
                    rows, cols = block_of(band, col)
                    total = (
                        kept[0, rows, cols].astype(jnp.float32) * own_scale
                        + came[rows, cols].astype(jnp.float32) * partner_scale
                    )
                    out[rows, cols] = total.astype(jnp.int32).astype(jnp.int16)

    block = (CHUNK, TILE_COLS)
    kept_block = (1, CHUNK, TILE_COLS)
    return call(
        kernel,
        (4,),
        [place, weights, own_exps, partner_exps],
        [
            (codes, kept_block, lambda t, p, *_: (0, chunk, 2 * ((1 - p[YHI]) * 4 + t) + p[KEEP])),
            (codes, kept_block, lambda t, p, *_: (0, chunk, 2 * (p[YHI] * 4 + t) + p[KEEP])),
            (received, block, lambda t, p, *_: (0, (1 - p[YHI]) * 4 + t)),
            (received, block, lambda t, p, *_: (0, p[YHI] * 4 + t)),
        ],
        [((CHUNK, 4 * TILE_COLS), jnp.int16, block, lambda t, *_: (0, t))] * 2,
    )


def add_fours(chunk, place, far_units, near_units, far, near):
    def kernel(place, far_units, near_units, far, near, *outs):
        z_to = lax.rem(place[SHIFT] + 4 - pl.program_id(0), 4)
        y_lo = place[YHI + 0]
        first = (place[6] * 8 + z_to * 2 + place[KEEP]) * SPAN
        for slot, out in enumerate(outs):

            @pl.when(pl.program_id(0) == slot)
            def _():
                for col in range(SPAN):
                    odds = []
                    for band in range(BANDS):
                        far_unit = far_units[chunk * BANDS + band, first + col]
                        near_unit = near_units[chunk * BANDS + band, first + col]
                        unit = jnp.minimum(far_unit, near_unit)
                        rows, cols = block_of(band, col)
                        total = (far[rows, cols].astype(jnp.int32) << (far_unit - unit)) + (
                            near[rows, cols].astype(jnp.int32) << (near_unit - unit)
                        )
                        out[rows, cols] = (total >> 1).astype(jnp.int16)
                        odd = total & 1
                        packed = odd[0:8]
                        for group in range(1, 16):
                            packed = packed | (odd[8 * group : 8 * group + 8] << group)
                        odds.append(packed)
                    out[pl.ds(CHUNK, EXTRA), pl.ds(col * BLOCK, BLOCK)] = jnp.concatenate(
                        odds, axis=0
                    ).astype(jnp.int16)

    block = (CHUNK, TILE_COLS)
    sent = (CHUNK + EXTRA, TILE_COLS)
    z_block = lambda t, p, *_: (0, lax.rem(p[SHIFT] + 4 - t, 4))
    return call(
        kernel,
        (4,),
        [place, far_units, near_units],
        [(far, block, z_block), (near, block, z_block)],
        [(sent, jnp.int16, sent, lambda t, *_: (0, 0))] * 4,
    )


def finish(place, denominator, units, parts):
    def kernel(place, denominator, *refs):
        units, refs = refs[:4], refs[4:]
        parts, (tiles, scales) = refs[: 4 * CHUNKS], refs[4 * CHUNKS :]
        chunk, half = pl.program_id(0), pl.program_id(1)
        divisor = jnp.full((1, 1), denominator[0], jnp.int32).astype(jnp.float32)
        core_rows = lax.rem(place[FLIP] + half, 2)
        first = place[7] * SPAN

        def fours(ref, unit, band, col):
            rows, cols = block_of(band, col)
            packed = ref[pl.ds(CHUNK, EXTRA), cols].astype(jnp.int32)[8 * band : 8 * band + 8]
            odd = jnp.concatenate([(packed >> group) & 1 for group in range(16)], axis=0)
            total = (ref[rows, cols].astype(jnp.int32) << 1) + odd
            return total.astype(jnp.float32) * ((1 << (unit + 8)).astype(jnp.float32) * (1.0 / 256))

        @pl.when((chunk == 0) & (half == 0))
        def _():
            scales[...] = jnp.zeros_like(scales)

        row_at = lax.broadcasted_iota(jnp.int32, scales.shape, 0)
        col_at = lax.broadcasted_iota(jnp.int32, scales.shape, 1)
        for c in range(CHUNKS):
            for h in range(2):

                @pl.when((chunk == c) & (half == h))
                def _():
                    found = scales[...]
                    for band in range(BANDS):
                        for col in range(SPAN):
                            at = (c * BANDS + band, first + col)
                            summed = fours(parts[4 * c + h], units[h][at], band, col) + fours(
                                parts[4 * c + h + 2], units[h + 2][at], band, col
                            )
                            largest = jnp.max(jnp.abs(summed), axis=(0, 1), keepdims=True)
                            scale = largest / divisor
                            rows, cols = block_of(band, col)
                            factor = 1.0 / (divisor * (scale + EPSILON))
                            tiles[rows, cols] = (summed * factor).astype(jnp.bfloat16)
                            here = (row_at == core_rows * 8 + c * BANDS + band) & (col_at == col)
                            found = jnp.where(here, scale, found)
                    scales[...] = found

    sent = (CHUNK + EXTRA, TILE_COLS)
    return call(
        kernel,
        (CHUNKS, 2),
        [place, denominator, *units],
        [(part, sent, lambda c, h, *_: (0, 0)) for part in parts],
        [
            (
                (2048, TILE_COLS),
                jnp.bfloat16,
                (CHUNK, TILE_COLS),
                lambda c, h, p, *_: (lax.rem(p[FLIP] + h, 2) * CHUNKS + c, 0),
            ),
            ((16, 4), jnp.float32, (16, 4), lambda c, h, *_: (0, 0)),
        ],
    )


def body(quant_codes, exponents, numerators, denominator):
    y_hi, x = jnp.divmod(lax.axis_index("ckpt"), 4)
    row = lax.axis_index("row")
    y_lo, z, core = row // 8, (row // 2) % 4, row % 2
    keep = (x + core) % 2
    place = jnp.stack(
        [
            y_hi * 4 + x,
            y_hi * 4 + (x + 1 - 2 * keep) % 4,
            keep,
            y_hi,
            (z - x) % 4,
            (x - z - core) % 2,
            y_lo,
            row,
        ]
    ).astype(jnp.int32)

    own_exps = exponents[0]
    partner_exps = lax.ppermute(own_exps, AXES, PAIR_PERM)
    pair_units = jnp.minimum(own_exps, partner_exps)
    far_units = lax.ppermute(pair_units, AXES, ACROSS_PERM)
    near_units = lax.ppermute(pair_units, AXES, BESIDE_PERM)
    four_units = jnp.minimum(far_units, near_units)
    units = [lax.ppermute(four_units, AXES, perm) for perm in ZX_PERMS]

    parts = []
    after = ()
    for chunk in range(CHUNKS):
        sent = pack(chunk, place, quant_codes, after)
        received = lax.ppermute(sent, AXES, PAIR_PERM)
        after = (received,)
        far, near = add_pairs(chunk, place, numerators, own_exps, partner_exps, quant_codes, received)
        far = lax.ppermute(far, AXES, ACROSS_PERM)
        near = lax.ppermute(near, AXES, BESIDE_PERM)
        slots = add_fours(chunk, place, far_units, near_units, far, near)
        slots = [lax.ppermute(slot, AXES, perm) for slot, perm in zip(slots, Z_PERMS)]
        slots = [lax.ppermute(slot, AXES, perm) for slot, perm in zip(slots, X_PERMS)]
        parts += slots
    return tuple(finish(place, denominator, units, parts))


def solution(mesh):
    placed = (P("ckpt", "row", None), P("ckpt", "row", None), P(), P())
    return jax.shard_map(
        body,
        mesh=mesh,
        in_specs=placed,
        out_specs=(P("ckpt", "row"), P("ckpt", "row")),
        check_vma=False,
    )
```

time: 896 us -> 324 us (0.36)
  blocking collectives: 372 us -> 0 us
  waiting for transfers between devices: 358 us -> 138 us
  starting transfers between devices: 0.04 us -> 130 us
  local copies, waits for them, and re-layouts: 104 us -> 0.75 us
  Pallas kernels: 0 us -> 47.7 us
  other arithmetic: 44.1 us -> 0.01 us
  between operations: 15.4 us -> 2.07 us
    all_to_all x1 -> x0, blocking collectives: 372 us -> none  [body(): lax.all_to_all(partial_rows, 'row', split_axis=1, concat_axis=0, tiled=True)]
    reduce_scatter x1 -> x0, waiting for transfers between devices: 358 us -> none  [body(): summed = lax.psum_scatter(relaid, 'ckpt', scatter_dimension=0, tiled=True)]
    ppermute x0 -> x51, waiting for transfers between devices: none -> 138 us  [the longest x4 48.9 us: body(): received = lax.ppermute(sent, AXES, PAIR_PERM)]
    ppermute x0 -> x51, starting transfers between devices: none -> 130 us  [the longest x32 89 us: body(): lax.ppermute(slot, AXES, perm)]
    mul x3 -> x0, local copies, waits for them, and re-layouts: 75.3 us -> none  [the longest x2 47.1 us: weigh_codes(): scaled = grid_values * powers_block[:, :, None, :, None]]
    pallas_call x0 -> x13, Pallas kernels: none -> 47.7 us  [call(): pl.pallas_call(whole, grid_spec=pltpu.PrefetchScalarGridSpec(num_scalar_p...]
    mul x2 -> x0, other arithmetic: 34.3 us -> none  [the longest x1 33.6 us: weigh_codes(): weighted = jnp.sum(own_weights[:, None, None, None, None] * scaled, axis=0)]
    unnamed x4, local copies, waits for them, and re-layouts: 21.8 us -> 0.01 us
  transfers between devices with their start and end apart: 1 -> 51, of which waited for: 1 -> 19; matrix products, arithmetic and copies ran while one was open for 0% -> 0% of each run, Pallas kernels for 0% -> 9%
where the time goes in v1:
time: 324 us; the launch traced here: 319 us
  waiting for transfers between devices  138 us (43%)
  starting transfers between devices  130 us (40%)
  Pallas kernels  47.7 us (15%)
    ppermute x32, starting transfers between devices, body(): lax.ppermute(slot, AXES, perm)  89 us
    ppermute x4, waiting for transfers between devices, body(): received = lax.ppermute(sent, AXES, PAIR_PERM)  48.9 us
    pallas_call x13, Pallas kernels, call(): pl.pallas_call(whole, grid_spec=pltpu.PrefetchScalarGridSpec(num_scalar_p...  47.7 us
    ppermute x32, waiting for transfers between devices, body(): lax.ppermute(slot, AXES, perm)  45 us
    ppermute x1, waiting for transfers between devices, body(): partner_exps = lax.ppermute(own_exps, AXES, PAIR_PERM)  24 us
    ppermute x4, starting transfers between devices, body(): units = [lax.ppermute(four_units, AXES, perm) for perm in ZX_PERMS]  16.8 us
    ppermute x4, waiting for transfers between devices, body(): units = [lax.ppermute(four_units, AXES, perm) for perm in ZX_PERMS]  10.3 us
    ppermute x4, starting transfers between devices, body(): far = lax.ppermute(far, AXES, ACROSS_PERM)  10.1 us
  transfers between devices with their start and end apart: 51, of which 19 were waited for; matrix products, arithmetic and copies ran while one was open for 0% of the time, Pallas kernels for 9%

profile of v1, /device:TPU:0, one launch (start us, length us, event | category | flops | bytes accessed | tf_op | source)
XLA Modules:
  0.0 318.6 jit_solution(7743811252075916064)
XLA Ops:
  0.8 4.7 %shard_map.59 = bf16[256,4096]{1,0:T(8,128)(2,1)S(1)} custom-call(s32[8]{0:T(128)S(1)} %stack.35.refs_0_, bf16[1,1024,8192]{2,1,0:T(8,128)(2,1)} %refs_5_.7), custom_call_target="tpu_custom_call" | custom-call | bytes 18874368 | tf_op jit(solution)/shard_map/pallas_call | solution.py:62
  7.2 24.5 %collective-permute-done.7.refs_6_.refs_7_.refs_2_ = bf16[256,4096]{1,0:T(8,128)(2,1)S(1)} collective-permute-done((bf16[256,4096]{1,0:T(8,128)(2,1)S(1)}, bf16[256,4096]{1,0:T(8,128)(2,1)S(1)}, u32[]{:S(2)}, u32[]{:S(2)}) %collective-permute-start.7) | collective-permute-done | bytes 2097184 | tf_op jit(solution)/shard_map/ppermute | solution.py:265
  31.6 4.7 %shard_map.62 = bf16[256,4096]{1,0:T(8,128)(2,1)S(1)} custom-call(s32[8]{0:T(128)S(1)} %stack.35.refs_0_, bf16[1,1024,8192]{2,1,0:T(8,128)(2,1)} %refs_5_.7, bf16[256,4096]{1,0:T(8,128)(2,1)S(1)} %collective-permute-done.7.refs_6_.refs_7_.refs_2_), custom_call_target="tpu_custom_call" | custom-call | bytes 18874368 | tf_op jit(solution)/shard_map/pallas_call | solution.py:62
  38.0 24.5 %collective-permute-done.18.refs_6_.refs_7_.refs_2_ = bf16[256,4096]{1,0:T(8,128)(2,1)S(1)} collective-permute-done((bf16[256,4096]{1,0:T(8,128)(2,1)S(1)}, bf16[256,4096]{1,0:T(8,128)(2,1)S(1)}, u32[]{:S(2)}, u32[]{:S(2)}) %collective-permute-start.18) | collective-permute-done | bytes 2097184 | tf_op jit(solution)/shard_map/ppermute | solution.py:265
  62.5 4.7 %shard_map.65 = bf16[256,4096]{1,0:T(8,128)(2,1)S(1)} custom-call(s32[8]{0:T(128)S(1)} %stack.35.refs_0_, bf16[1,1024,8192]{2,1,0:T(8,128)(2,1)} %refs_5_.7, bf16[256,4096]{1,0:T(8,128)(2,1)S(1)} %collective-permute-done.18.refs_6_.refs_7_.refs_2_), custom_call_target="tpu_custom_call" | custom-call | bytes 18874368 | tf_op jit(solution)/shard_map/pallas_call | solution.py:62
  69.3 24.0 %collective-permute-done.refs_3_ = s32[8,64]{1,0:T(8,128)S(1)} collective-permute-done((s32[8,64]{1,0:T(8,128)S(1)}, s32[8,64]{1,0:T(8,128)S(1)}, u32[]{:S(2)}, u32[]{:S(2)}) %collective-permute-start) | collective-permute-done | bytes 2080 | tf_op jit(solution)/shard_map/ppermute | solution.py:254
  93.3 3.9 %shard_map.60 = (s16[256,2048]{1,0:T(8,128)(2,1)S(1)}, s16[256,2048]{1,0:T(8,128)(2,1)S(1)}) custom-call(s32[8]{0:T(128)S(1)} %stack.35.refs_0_, s32[8]{0:T(128)S(1)} %copy-done.1, s32[8,64]{1,0:T(8,128)S(1)} %bitcast.11, s32[8,64]{1,0:T(8,128)S(1)} %collective-permute-done.refs_3_, bf16[1,1024,8192]{2,1,0:T(8,128)(2,1)} %refs_5_.7, ...), custom_call_target="tpu_custom_call" | custom-call | bytes 39845888 | tf_op jit(solution)/shard_map/pallas_call | solution.py:62
  99.8 4.7 %shard_map.68 = bf16[256,4096]{1,0:T(8,128)(2,1)S(1)} custom-call(s32[8]{0:T(128)S(1)} %stack.35.refs_0_, bf16[1,1024,8192]{2,1,0:T(8,128)(2,1)} %refs_5_.7, bf16[256,4096]{1,0:T(8,128)(2,1)S(1)} %collective-permute-done.29.refs_6_.refs_7_.refs_2_), custom_call_target="tpu_custom_call" | custom-call | bytes 18874368 | tf_op jit(solution)/shard_map/pallas_call | solution.py:62
  106.0 3.5 %collective-permute-start.1 = (s32[8,64]{1,0:T(8,128)S(1)}, s32[8,64]{1,0:T(8,128)S(1)}, u32[]{:S(2)}, u32[]{:S(2)}) collective-permute-start(s32[8,64]{1,0:T(8,128)S(1)} %bitcast_minimum_fusion), channel_id=1, source_target_pairs={{0,8},{1,9},{2,10},{3,11},{4,12},{5,13},{6,14},{7,15},{8,72},{9,73... | collective-permute-start | bytes 6152 | tf_op jit(solution)/shard_map/ppermute | solution.py:256
  110.2 4.0 %shard_map.63 = (s16[256,2048]{1,0:T(8,128)(2,1)S(1)}, s16[256,2048]{1,0:T(8,128)(2,1)S(1)}) custom-call(s32[8]{0:T(128)S(1)} %stack.35.refs_0_, s32[8]{0:T(128)S(1)} %copy-done.1, s32[8,64]{1,0:T(8,128)S(1)} %bitcast.12, s32[8,64]{1,0:T(8,128)S(1)} %collective-permute-done.refs_3_, bf16[1,1024,8192]{2,1,0:T(8,128)(2,1)} %refs_5_.7, ...), custom_call_target="tpu_custom_call" | custom-call | bytes 39845888 | tf_op jit(solution)/shard_map/pallas_call | solution.py:62
  114.1 9.9 %collective-permute-done.1.refs_1_ = s32[8,64]{1,0:T(8,128)S(1)} collective-permute-done((s32[8,64]{1,0:T(8,128)S(1)}, s32[8,64]{1,0:T(8,128)S(1)}, u32[]{:S(2)}, u32[]{:S(2)}) %collective-permute-start.1) | collective-permute-done | bytes 2080 | tf_op jit(solution)/shard_map/ppermute | solution.py:256
  128.1 10.6 %collective-permute-start.4 = (s32[8,64]{1,0:T(8,128)S(1)}, s32[8,64]{1,0:T(8,128)S(1)}, u32[]{:S(2)}, u32[]{:S(2)}) collective-permute-start(s32[8,64]{1,0:T(8,128)S(1)} %min.7), channel_id=1, source_target_pairs={{0,6},{1,7},{2,16},{3,17},{4,34},{5,35},{6,52},{7,53},{8,14},{9,15... | collective-permute-start | bytes 6152 | tf_op jit(solution)/shard_map/ppermute | solution.py:259
  138.7 3.8 %collective-permute-done.4.refs_3_ = s32[8,64]{1,0:T(8,128)S(1)} collective-permute-done((s32[8,64]{1,0:T(8,128)S(1)}, s32[8,64]{1,0:T(8,128)S(1)}, u32[]{:S(2)}, u32[]{:S(2)}) %collective-permute-start.4) | collective-permute-done | bytes 2080 | tf_op jit(solution)/shard_map/ppermute | solution.py:259
  142.5 5.6 %collective-permute-start.5 = (s32[8,64]{1,0:T(8,128)S(1)}, s32[8,64]{1,0:T(8,128)S(1)}, u32[]{:S(2)}, u32[]{:S(2)}) collective-permute-start(s32[8,64]{1,0:T(8,128)S(1)} %min.7), channel_id=1, source_target_pairs={{0,4},{1,5},{2,22},{3,23},{4,32},{5,33},{6,50},{7,51},{8,12},{9,13... | collective-permute-start | bytes 6152 | tf_op jit(solution)/shard_map/ppermute | solution.py:259
  149.5 5.1 %collective-permute-done.6.refs_5_ = s32[8,64]{1,0:T(8,128)S(1)} collective-permute-done((s32[8,64]{1,0:T(8,128)S(1)}, s32[8,64]{1,0:T(8,128)S(1)}, u32[]{:S(2)}, u32[]{:S(2)}) %collective-permute-start.6) | collective-permute-done | bytes 2080 | tf_op jit(solution)/shard_map/ppermute | solution.py:259
  154.6 10.0 %collective-permute-start.12 = (s16[272,512]{1,0:T(8,128)(2,1)S(1)}, s16[272,512]{1,0:T(8,128)(2,1)S(1)}, u32[]{:S(2)}, u32[]{:S(2)}) collective-permute-start(s16[272,512]{1,0:T(8,128)(2,1)S(1)} %get-tuple-element.29), channel_id=1, source_target_pairs={{0,6},{1,7},{2,0},{3,1},{4,2},{5,3},{6,4},{7,5},{8,14},{9,15},{10,... | collective-permute-start | bytes 835592 | tf_op jit(solution)/shard_map/ppermute | solution.py:271
  164.6 1.9 collective-permute-start.14
  166.5 6.1 %collective-permute-done.12 = s16[272,512]{1,0:T(8,128)(2,1)S(1)} collective-permute-done((s16[272,512]{1,0:T(8,128)(2,1)S(1)}, s16[272,512]{1,0:T(8,128)(2,1)S(1)}, u32[]{:S(2)}, u32[]{:S(2)}) %collective-permute-start.12) | collective-permute-done | bytes 278560 | tf_op jit(solution)/shard_map/ppermute | solution.py:271
  175.3 4.0 %shard_map.66 = (s16[256,2048]{1,0:T(8,128)(2,1)S(1)}, s16[256,2048]{1,0:T(8,128)(2,1)S(1)}) custom-call(s32[8]{0:T(128)S(1)} %stack.35.refs_0_, s32[8]{0:T(128)S(1)} %copy-done.1, s32[8,64]{1,0:T(8,128)S(1)} %bitcast.13, s32[8,64]{1,0:T(8,128)S(1)} %collective-permute-done.refs_3_, bf16[1,1024,8192]{2,1,0:T(8,128)(2,1)} %refs_5_.7, ...), custom_call_target="tpu_custom_call" | custom-call | bytes 39845888 | tf_op jit(solution)/shard_map/pallas_call | solution.py:62
  179.2 3.4 %collective-permute-done.16 = s16[272,512]{1,0:T(8,128)(2,1)S(1)} collective-permute-done((s16[272,512]{1,0:T(8,128)(2,1)S(1)}, s16[272,512]{1,0:T(8,128)(2,1)S(1)}, u32[]{:S(2)}, u32[]{:S(2)}) %collective-permute-start.16) | collective-permute-done | bytes 278560 | tf_op jit(solution)/shard_map/ppermute | solution.py:271
  182.6 4.9 %collective-permute-start.30 = (s16[256,2048]{1,0:T(8,128)(2,1)S(1)}, s16[256,2048]{1,0:T(8,128)(2,1)S(1)}, u32[]{:S(2)}, u32[]{:S(2)}) collective-permute-start(s16[256,2048]{1,0:T(8,128)(2,1)S(1)} %get-tuple-element.38), channel_id=1, source_target_pairs={{0,8},{1,9},{2,10},{3,11},{4,12},{5,13},{6,14},{7,15},{8,72},{9,73... | collective-permute-start | bytes 3145736 | tf_op jit(solution)/shard_map/ppermute | solution.py:268
  188.2 1.9 collective-permute-start.13
  190.2 1.9 collective-permute-start.15
  193.9 9.4 %collective-permute-done.13.refs_7_ = s16[272,512]{1,0:T(8,128)(2,1)S(1)} collective-permute-done((s16[272,512]{1,0:T(8,128)(2,1)S(1)}, s16[272,512]{1,0:T(8,128)(2,1)S(1)}, u32[]{:S(2)}, u32[]{:S(2)}) %collective-permute-start.13) | collective-permute-done | bytes 278560 | tf_op jit(solution)/shard_map/ppermute | solution.py:272
  203.3 1.9 collective-permute-start.17
  205.9 1.9 collective-permute-start.23
  207.8 4.0 %shard_map.69 = (s16[256,2048]{1,0:T(8,128)(2,1)S(1)}, s16[256,2048]{1,0:T(8,128)(2,1)S(1)}) custom-call(s32[8]{0:T(128)S(1)} %stack.35.refs_0_, s32[8]{0:T(128)S(1)} %copy-done.1, s32[8,64]{1,0:T(8,128)S(1)} %bitcast.14, s32[8,64]{1,0:T(8,128)S(1)} %collective-permute-done.refs_3_, bf16[1,1024,8192]{2,1,0:T(8,128)(2,1)} %refs_5_.7, ...), custom_call_target="tpu_custom_call" | custom-call | bytes 39845888 | tf_op jit(solution)/shard_map/pallas_call | solution.py:62
  211.8 3.4 %collective-permute-start.41 = (s16[256,2048]{1,0:T(8,128)(2,1)S(1)}, s16[256,2048]{1,0:T(8,128)(2,1)S(1)}, u32[]{:S(2)}, u32[]{:S(2)}) collective-permute-start(s16[256,2048]{1,0:T(8,128)(2,1)S(1)} %get-tuple-element.44), channel_id=1, source_target_pairs={{0,8},{1,9},{2,10},{3,11},{4,12},{5,13},{6,14},{7,15},{8,72},{9,73... | collective-permute-start | bytes 3145736 | tf_op jit(solution)/shard_map/ppermute | solution.py:268
  216.0 4.4 %collective-permute-start.25 = (s16[272,512]{1,0:T(8,128)(2,1)S(1)}, s16[272,512]{1,0:T(8,128)(2,1)S(1)}, u32[]{:S(2)}, u32[]{:S(2)}) collective-permute-start(s16[272,512]{1,0:T(8,128)(2,1)S(1)} %get-tuple-element.36), channel_id=1, source_target_pairs={{0,4},{1,5},{2,6},{3,7},{4,0},{5,1},{6,2},{7,3},{8,12},{9,13},{10,... | collective-permute-start | bytes 835592 | tf_op jit(solution)/shard_map/ppermute | solution.py:271
  220.3 7.5 %collective-permute-done.25 = s16[272,512]{1,0:T(8,128)(2,1)S(1)} collective-permute-done((s16[272,512]{1,0:T(8,128)(2,1)S(1)}, s16[272,512]{1,0:T(8,128)(2,1)S(1)}, u32[]{:S(2)}, u32[]{:S(2)}) %collective-permute-start.25) | collective-permute-done | bytes 278560 | tf_op jit(solution)/shard_map/ppermute | solution.py:271
  230.4 6.9 %collective-permute-start.24 = (s16[272,512]{1,0:T(8,128)(2,1)S(1)}, s16[272,512]{1,0:T(8,128)(2,1)S(1)}, u32[]{:S(2)}, u32[]{:S(2)}) collective-permute-start(s16[272,512]{1,0:T(8,128)(2,1)S(1)} %collective-permute-done.23), channel_id=1, source_target_pairs={{0,16},{1,17},{2,34},{3,35},{4,52},{5,53},{6,6},{7,7},{8,24},{9,25... | collective-permute-start | bytes 835592 | tf_op jit(solution)/shard_map/ppermute | solution.py:272
  239.1 1.9 collective-permute-start.26
  241.8 2.5 collective-permute-done.24.refs_11_
  246.2 5.1 %collective-permute-done.26.refs_12_ = s16[272,512]{1,0:T(8,128)(2,1)S(1)} collective-permute-done((s16[272,512]{1,0:T(8,128)(2,1)S(1)}, s16[272,512]{1,0:T(8,128)(2,1)S(1)}, u32[]{:S(2)}, u32[]{:S(2)}) %collective-permute-start.26) | collective-permute-done | bytes 278560 | tf_op jit(solution)/shard_map/ppermute | solution.py:272
  251.3 3.7 %collective-permute-start.36 = (s16[272,512]{1,0:T(8,128)(2,1)S(1)}, s16[272,512]{1,0:T(8,128)(2,1)S(1)}, u32[]{:S(2)}, u32[]{:S(2)}) collective-permute-start(s16[272,512]{1,0:T(8,128)(2,1)S(1)} %get-tuple-element.42), channel_id=1, source_target_pairs={{0,4},{1,5},{2,6},{3,7},{4,0},{5,1},{6,2},{7,3},{8,12},{9,13},{10,... | collective-permute-start | bytes 835592 | tf_op jit(solution)/shard_map/ppermute | solution.py:271
  255.0 3.0 collective-permute-start.28
  258.5 8.9 %collective-permute-start.38 = (s16[272,512]{1,0:T(8,128)(2,1)S(1)}, s16[272,512]{1,0:T(8,128)(2,1)S(1)}, u32[]{:S(2)}, u32[]{:S(2)}) collective-permute-start(s16[272,512]{1,0:T(8,128)(2,1)S(1)} %get-tuple-element.43), channel_id=1, source_target_pairs={{0,2},{1,3},{2,4},{3,5},{4,6},{5,7},{6,0},{7,1},{8,10},{9,11},{10,... | collective-permute-start | bytes 835592 | tf_op jit(solution)/shard_map/ppermute | solution.py:271
  268.3 1.9 collective-permute-start.35
  272.1 1.9 collective-permute-start.37
  274.7 1.9 collective-permute-start.45
  276.6 7.0 %collective-permute-start.47 = (s16[272,512]{1,0:T(8,128)(2,1)S(1)}, s16[272,512]{1,0:T(8,128)(2,1)S(1)}, u32[]{:S(2)}, u32[]{:S(2)}) collective-permute-start(s16[272,512]{1,0:T(8,128)(2,1)S(1)} %get-tuple-element.48), channel_id=1, source_target_pairs={{0,4},{1,5},{2,6},{3,7},{4,0},{5,1},{6,2},{7,3},{8,12},{9,13},{10,... | collective-permute-start | bytes 835592 | tf_op jit(solution)/shard_map/ppermute | solution.py:271
  285.4 3.3 %collective-permute-start.49 = (s16[272,512]{1,0:T(8,128)(2,1)S(1)}, s16[272,512]{1,0:T(8,128)(2,1)S(1)}, u32[]{:S(2)}, u32[]{:S(2)}) collective-permute-start(s16[272,512]{1,0:T(8,128)(2,1)S(1)} %get-tuple-element.49), channel_id=1, source_target_pairs={{0,2},{1,3},{2,4},{3,5},{4,6},{5,7},{6,0},{7,1},{8,10},{9,11},{10,... | collective-permute-start | bytes 835592 | tf_op jit(solution)/shard_map/ppermute | solution.py:271
  288.6 2.7 collective-permute-start.39
  292.1 4.5 %collective-permute-start.46 = (s16[272,512]{1,0:T(8,128)(2,1)S(1)}, s16[272,512]{1,0:T(8,128)(2,1)S(1)}, u32[]{:S(2)}, u32[]{:S(2)}) collective-permute-start(s16[272,512]{1,0:T(8,128)(2,1)S(1)} %collective-permute-done.45), channel_id=1, source_target_pairs={{0,16},{1,17},{2,34},{3,35},{4,52},{5,53},{6,6},{7,7},{8,24},{9,25... | collective-permute-start | bytes 835592 | tf_op jit(solution)/shard_map/ppermute | solution.py:272
  296.6 3.3 %collective-permute-start.48 = (s16[272,512]{1,0:T(8,128)(2,1)S(1)}, s16[272,512]{1,0:T(8,128)(2,1)S(1)}, u32[]{:S(2)}, u32[]{:S(2)}) collective-permute-start(s16[272,512]{1,0:T(8,128)(2,1)S(1)} %collective-permute-done.47), channel_id=1, source_target_pairs={{0,32},{1,33},{2,50},{3,51},{4,4},{5,5},{6,22},{7,23},{8,40},{9,41... | collective-permute-start | bytes 835592 | tf_op jit(solution)/shard_map/ppermute | solution.py:272
  299.9 2.8 collective-permute-start.50
  304.2 6.3 %collective-permute-done.48.refs_20_ = s16[272,512]{1,0:T(8,128)(2,1)S(1)} collective-permute-done((s16[272,512]{1,0:T(8,128)(2,1)S(1)}, s16[272,512]{1,0:T(8,128)(2,1)S(1)}, u32[]{:S(2)}, u32[]{:S(2)}) %collective-permute-start.48) | collective-permute-done | bytes 278560 | tf_op jit(solution)/shard_map/ppermute | solution.py:272
  312.0 6.0 %shard_map.71 = (bf16[2048,512]{1,0:T(8,128)(2,1)}, f32[16,4]{1,0:T(8,128)S(1)}) custom-call(s32[8]{0:T(128)S(1)} %stack.35.refs_0_, s32[1]{0:T(128)S(6)} %copy.7.refs_1_, s32[8,64]{1,0:T(8,128)S(1)} %collective-permute-done.3.refs_2_, s32[8,64]{1,0:T(8,128)S(1)} %collective-permute-done.4.refs_3_, s32[8,64]{1,0:T(8,128)S(1)} %collective-permute-done.5.refs_4_, ...), custom_call_target="tpu_custom_call" | custom-call | bytes 6553856 | tf_op jit(solution)/shard_map/pallas_call | solution.py:62
  (75 shorter events, 38.5 us)
Async XLA Ops:
  5.5 26.1 %collective-permute-start.7 = (bf16[256,4096]{1,0:T(8,128)(2,1)S(1)}, bf16[256,4096]{1,0:T(8,128)(2,1)S(1)}, u32[]{:S(2)}, u32[]{:S(2)}) collective-permute-start(bf16[256,4096]{1,0:T(8,128)(2,1)S(1)} %shard_map.59), channel_id=1, source_target_pairs={{0,16},{1,49},{2,18},{3,51},{4,20},{5,53},{6,22},{7,55},{8,24},{9,... | collective-permute-start | bytes 6291464 | tf_op jit(solution)/shard_map/ppermute | solution.py:265
  36.4 26.1 %collective-permute-start.18 = (bf16[256,4096]{1,0:T(8,128)(2,1)S(1)}, bf16[256,4096]{1,0:T(8,128)(2,1)S(1)}, u32[]{:S(2)}, u32[]{:S(2)}) collective-permute-start(bf16[256,4096]{1,0:T(8,128)(2,1)S(1)} %shard_map.62), channel_id=1, source_target_pairs={{0,16},{1,49},{2,18},{3,51},{4,20},{5,53},{6,22},{7,55},{8,24},{9,... | collective-permute-start | bytes 6291464 | tf_op jit(solution)/shard_map/ppermute | solution.py:265
  67.2 32.6 %collective-permute-start.29 = (bf16[256,4096]{1,0:T(8,128)(2,1)S(1)}, bf16[256,4096]{1,0:T(8,128)(2,1)S(1)}, u32[]{:S(2)}, u32[]{:S(2)}) collective-permute-start(bf16[256,4096]{1,0:T(8,128)(2,1)S(1)} %shard_map.65), channel_id=1, source_target_pairs={{0,16},{1,49},{2,18},{3,51},{4,20},{5,53},{6,22},{7,55},{8,24},{9,... | collective-permute-start | bytes 6291464 | tf_op jit(solution)/shard_map/ppermute | solution.py:265
  68.8 24.5 %collective-permute-start = (s32[8,64]{1,0:T(8,128)S(1)}, s32[8,64]{1,0:T(8,128)S(1)}, u32[]{:S(2)}, u32[]{:S(2)}) collective-permute-start(s32[8,64]{1,0:T(8,128)S(1)} %bitcast.10), channel_id=1, source_target_pairs={{0,16},{1,49},{2,18},{3,51},{4,20},{5,53},{6,22},{7,55},{8,24},{9,... | collective-permute-start | bytes 6152 | tf_op jit(solution)/shard_map/ppermute | solution.py:254
  97.3 27.6 %collective-permute-start.8 = (s16[256,2048]{1,0:T(8,128)(2,1)S(1)}, s16[256,2048]{1,0:T(8,128)(2,1)S(1)}, u32[]{:S(2)}, u32[]{:S(2)}) collective-permute-start(s16[256,2048]{1,0:T(8,128)(2,1)S(1)} %get-tuple-element.26), channel_id=1, source_target_pairs={{0,8},{1,9},{2,10},{3,11},{4,12},{5,13},{6,14},{7,15},{8,72},{9,73... | collective-permute-start | bytes 3145736 | tf_op jit(solution)/shard_map/ppermute | solution.py:268
  99.0 25.9 %collective-permute-start.9 = (s16[256,2048]{1,0:T(8,128)(2,1)S(1)}, s16[256,2048]{1,0:T(8,128)(2,1)S(1)}, u32[]{:S(2)}, u32[]{:S(2)}) collective-permute-start(s16[256,2048]{1,0:T(8,128)(2,1)S(1)} %get-tuple-element.27), channel_id=1, source_target_pairs={{0,0},{1,1},{2,2},{3,3},{4,4},{5,5},{6,6},{7,7},{8,64},{9,65},{10,... | collective-permute-start | bytes 3145736 | tf_op jit(solution)/shard_map/ppermute | solution.py:269
  104.5 101.5 %collective-permute-start.40 = (bf16[256,4096]{1,0:T(8,128)(2,1)S(1)}, bf16[256,4096]{1,0:T(8,128)(2,1)S(1)}, u32[]{:S(2)}, u32[]{:S(2)}) collective-permute-start(bf16[256,4096]{1,0:T(8,128)(2,1)S(1)} %shard_map.68), channel_id=1, source_target_pairs={{0,16},{1,49},{2,18},{3,51},{4,20},{5,53},{6,22},{7,55},{8,24},{9,... | collective-permute-start | bytes 6291464 | tf_op jit(solution)/shard_map/ppermute | solution.py:265
  106.0 18.0 %collective-permute-start.1 = (s32[8,64]{1,0:T(8,128)S(1)}, s32[8,64]{1,0:T(8,128)S(1)}, u32[]{:S(2)}, u32[]{:S(2)}) collective-permute-start(s32[8,64]{1,0:T(8,128)S(1)} %bitcast_minimum_fusion), channel_id=1, source_target_pairs={{0,8},{1,9},{2,10},{3,11},{4,12},{5,13},{6,14},{7,15},{8,72},{9,73... | collective-permute-start | bytes 6152 | tf_op jit(solution)/shard_map/ppermute | solution.py:256
  109.5 14.7 %collective-permute-start.2 = (s32[8,64]{1,0:T(8,128)S(1)}, s32[8,64]{1,0:T(8,128)S(1)}, u32[]{:S(2)}, u32[]{:S(2)}) collective-permute-start(s32[8,64]{1,0:T(8,128)S(1)} %bitcast_minimum_fusion), channel_id=1, source_target_pairs={{0,0},{1,1},{2,2},{3,3},{4,4},{5,5},{6,6},{7,7},{8,64},{9,65},{10,... | collective-permute-start | bytes 6152 | tf_op jit(solution)/shard_map/ppermute | solution.py:257
  124.1 64.2 %collective-permute-start.19 = (s16[256,2048]{1,0:T(8,128)(2,1)S(1)}, s16[256,2048]{1,0:T(8,128)(2,1)S(1)}, u32[]{:S(2)}, u32[]{:S(2)}) collective-permute-start(s16[256,2048]{1,0:T(8,128)(2,1)S(1)} %get-tuple-element.32), channel_id=1, source_target_pairs={{0,8},{1,9},{2,10},{3,11},{4,12},{5,13},{6,14},{7,15},{8,72},{9,73... | collective-permute-start | bytes 3145736 | tf_op jit(solution)/shard_map/ppermute | solution.py:268
  124.2 66.0 %collective-permute-start.20 = (s16[256,2048]{1,0:T(8,128)(2,1)S(1)}, s16[256,2048]{1,0:T(8,128)(2,1)S(1)}, u32[]{:S(2)}, u32[]{:S(2)}) collective-permute-start(s16[256,2048]{1,0:T(8,128)(2,1)S(1)} %get-tuple-element.33), channel_id=1, source_target_pairs={{0,0},{1,1},{2,2},{3,3},{4,4},{5,5},{6,6},{7,7},{8,64},{9,65},{10,... | collective-permute-start | bytes 3145736 | tf_op jit(solution)/shard_map/ppermute | solution.py:269
  126.7 37.8 %collective-permute-start.10 = (s16[272,512]{1,0:T(8,128)(2,1)S(1)}, s16[272,512]{1,0:T(8,128)(2,1)S(1)}, u32[]{:S(2)}, u32[]{:S(2)}) collective-permute-start(s16[272,512]{1,0:T(8,128)(2,1)S(1)} %get-tuple-element.28), channel_id=1, source_target_pairs={{0,0},{1,1},{2,2},{3,3},{4,4},{5,5},{6,6},{7,7},{8,8},{9,9},{10,10... | collective-permute-start | bytes 835592 | tf_op jit(solution)/shard_map/ppermute | solution.py:271
  128.1 14.3 %collective-permute-start.4 = (s32[8,64]{1,0:T(8,128)S(1)}, s32[8,64]{1,0:T(8,128)S(1)}, u32[]{:S(2)}, u32[]{:S(2)}) collective-permute-start(s32[8,64]{1,0:T(8,128)S(1)} %min.7), channel_id=1, source_target_pairs={{0,6},{1,7},{2,16},{3,17},{4,34},{5,35},{6,52},{7,53},{8,14},{9,15... | collective-permute-start | bytes 6152 | tf_op jit(solution)/shard_map/ppermute | solution.py:259
  154.6 18.0 %collective-permute-start.12 = (s16[272,512]{1,0:T(8,128)(2,1)S(1)}, s16[272,512]{1,0:T(8,128)(2,1)S(1)}, u32[]{:S(2)}, u32[]{:S(2)}) collective-permute-start(s16[272,512]{1,0:T(8,128)(2,1)S(1)} %get-tuple-element.29), channel_id=1, source_target_pairs={{0,6},{1,7},{2,0},{3,1},{4,2},{5,3},{6,4},{7,5},{8,14},{9,15},{10,... | collective-permute-start | bytes 835592 | tf_op jit(solution)/shard_map/ppermute | solution.py:271
  164.6 10.0 %collective-permute-start.14 = (s16[272,512]{1,0:T(8,128)(2,1)S(1)}, s16[272,512]{1,0:T(8,128)(2,1)S(1)}, u32[]{:S(2)}, u32[]{:S(2)}) collective-permute-start(s16[272,512]{1,0:T(8,128)(2,1)S(1)} %get-tuple-element.30), channel_id=1, source_target_pairs={{0,4},{1,5},{2,6},{3,7},{4,0},{5,1},{6,2},{7,3},{8,12},{9,13},{10,... | collective-permute-start | bytes 835592 | tf_op jit(solution)/shard_map/ppermute | solution.py:271
  172.5 10.1 %collective-permute-start.16 = (s16[272,512]{1,0:T(8,128)(2,1)S(1)}, s16[272,512]{1,0:T(8,128)(2,1)S(1)}, u32[]{:S(2)}, u32[]{:S(2)}) collective-permute-start(s16[272,512]{1,0:T(8,128)(2,1)S(1)} %get-tuple-element.31), channel_id=1, source_target_pairs={{0,2},{1,3},{2,4},{3,5},{4,6},{5,7},{6,0},{7,1},{8,10},{9,11},{10,... | collective-permute-start | bytes 835592 | tf_op jit(solution)/shard_map/ppermute | solution.py:271
  174.6 12.9 %collective-permute-start.11 = (s16[272,512]{1,0:T(8,128)(2,1)S(1)}, s16[272,512]{1,0:T(8,128)(2,1)S(1)}, u32[]{:S(2)}, u32[]{:S(2)}) collective-permute-start(s16[272,512]{1,0:T(8,128)(2,1)S(1)} %collective-permute-done.10), channel_id=1, source_target_pairs={{0,0},{1,1},{2,18},{3,19},{4,36},{5,37},{6,54},{7,55},{8,8},{9,9},... | collective-permute-start | bytes 835592 | tf_op jit(solution)/shard_map/ppermute | solution.py:272
  182.6 47.1 %collective-permute-start.30 = (s16[256,2048]{1,0:T(8,128)(2,1)S(1)}, s16[256,2048]{1,0:T(8,128)(2,1)S(1)}, u32[]{:S(2)}, u32[]{:S(2)}) collective-permute-start(s16[256,2048]{1,0:T(8,128)(2,1)S(1)} %get-tuple-element.38), channel_id=1, source_target_pairs={{0,8},{1,9},{2,10},{3,11},{4,12},{5,13},{6,14},{7,15},{8,72},{9,73... | collective-permute-start | bytes 3145736 | tf_op jit(solution)/shard_map/ppermute | solution.py:268
  187.5 42.9 %collective-permute-start.31 = (s16[256,2048]{1,0:T(8,128)(2,1)S(1)}, s16[256,2048]{1,0:T(8,128)(2,1)S(1)}, u32[]{:S(2)}, u32[]{:S(2)}) collective-permute-start(s16[256,2048]{1,0:T(8,128)(2,1)S(1)} %get-tuple-element.39), channel_id=1, source_target_pairs={{0,0},{1,1},{2,2},{3,3},{4,4},{5,5},{6,6},{7,7},{8,64},{9,65},{10,... | collective-permute-start | bytes 3145736 | tf_op jit(solution)/shard_map/ppermute | solution.py:269
  188.2 15.0 %collective-permute-start.13 = (s16[272,512]{1,0:T(8,128)(2,1)S(1)}, s16[272,512]{1,0:T(8,128)(2,1)S(1)}, u32[]{:S(2)}, u32[]{:S(2)}) collective-permute-start(s16[272,512]{1,0:T(8,128)(2,1)S(1)} %collective-permute-done.12), channel_id=1, source_target_pairs={{0,16},{1,17},{2,34},{3,35},{4,52},{5,53},{6,6},{7,7},{8,24},{9,25... | collective-permute-start | bytes 835592 | tf_op jit(solution)/shard_map/ppermute | solution.py:272
  190.2 15.0 %collective-permute-start.15 = (s16[272,512]{1,0:T(8,128)(2,1)S(1)}, s16[272,512]{1,0:T(8,128)(2,1)S(1)}, u32[]{:S(2)}, u32[]{:S(2)}) collective-permute-start(s16[272,512]{1,0:T(8,128)(2,1)S(1)} %collective-permute-done.14), channel_id=1, source_target_pairs={{0,32},{1,33},{2,50},{3,51},{4,4},{5,5},{6,22},{7,23},{8,40},{9,41... | collective-permute-start | bytes 835592 | tf_op jit(solution)/shard_map/ppermute | solution.py:272
  203.3 8.5 %collective-permute-start.17 = (s16[272,512]{1,0:T(8,128)(2,1)S(1)}, s16[272,512]{1,0:T(8,128)(2,1)S(1)}, u32[]{:S(2)}, u32[]{:S(2)}) collective-permute-start(s16[272,512]{1,0:T(8,128)(2,1)S(1)} %collective-permute-done.16), channel_id=1, source_target_pairs={{0,48},{1,49},{2,2},{3,3},{4,20},{5,21},{6,38},{7,39},{8,56},{9,57... | collective-permute-start | bytes 835592 | tf_op jit(solution)/shard_map/ppermute | solution.py:272
  205.2 10.0 %collective-permute-start.21 = (s16[272,512]{1,0:T(8,128)(2,1)S(1)}, s16[272,512]{1,0:T(8,128)(2,1)S(1)}, u32[]{:S(2)}, u32[]{:S(2)}) collective-permute-start(s16[272,512]{1,0:T(8,128)(2,1)S(1)} %get-tuple-element.34), channel_id=1, source_target_pairs={{0,0},{1,1},{2,2},{3,3},{4,4},{5,5},{6,6},{7,7},{8,8},{9,9},{10,10... | collective-permute-start | bytes 835592 | tf_op jit(solution)/shard_map/ppermute | solution.py:271
  205.9 10.0 %collective-permute-start.23 = (s16[272,512]{1,0:T(8,128)(2,1)S(1)}, s16[272,512]{1,0:T(8,128)(2,1)S(1)}, u32[]{:S(2)}, u32[]{:S(2)}) collective-permute-start(s16[272,512]{1,0:T(8,128)(2,1)S(1)} %get-tuple-element.35), channel_id=1, source_target_pairs={{0,6},{1,7},{2,0},{3,1},{4,2},{5,3},{6,4},{7,5},{8,14},{9,15},{10,... | collective-permute-start | bytes 835592 | tf_op jit(solution)/shard_map/ppermute | solution.py:271
  211.8 55.6 %collective-permute-start.41 = (s16[256,2048]{1,0:T(8,128)(2,1)S(1)}, s16[256,2048]{1,0:T(8,128)(2,1)S(1)}, u32[]{:S(2)}, u32[]{:S(2)}) collective-permute-start(s16[256,2048]{1,0:T(8,128)(2,1)S(1)} %get-tuple-element.44), channel_id=1, source_target_pairs={{0,8},{1,9},{2,10},{3,11},{4,12},{5,13},{6,14},{7,15},{8,72},{9,73... | collective-permute-start | bytes 3145736 | tf_op jit(solution)/shard_map/ppermute | solution.py:268
  215.2 53.1 %collective-permute-start.42 = (s16[256,2048]{1,0:T(8,128)(2,1)S(1)}, s16[256,2048]{1,0:T(8,128)(2,1)S(1)}, u32[]{:S(2)}, u32[]{:S(2)}) collective-permute-start(s16[256,2048]{1,0:T(8,128)(2,1)S(1)} %get-tuple-element.45), channel_id=1, source_target_pairs={{0,0},{1,1},{2,2},{3,3},{4,4},{5,5},{6,6},{7,7},{8,64},{9,65},{10,... | collective-permute-start | bytes 3145736 | tf_op jit(solution)/shard_map/ppermute | solution.py:269
  216.0 11.9 %collective-permute-start.25 = (s16[272,512]{1,0:T(8,128)(2,1)S(1)}, s16[272,512]{1,0:T(8,128)(2,1)S(1)}, u32[]{:S(2)}, u32[]{:S(2)}) collective-permute-start(s16[272,512]{1,0:T(8,128)(2,1)S(1)} %get-tuple-element.36), channel_id=1, source_target_pairs={{0,4},{1,5},{2,6},{3,7},{4,0},{5,1},{6,2},{7,3},{8,12},{9,13},{10,... | collective-permute-start | bytes 835592 | tf_op jit(solution)/shard_map/ppermute | solution.py:271
  227.8 11.3 %collective-permute-start.27 = (s16[272,512]{1,0:T(8,128)(2,1)S(1)}, s16[272,512]{1,0:T(8,128)(2,1)S(1)}, u32[]{:S(2)}, u32[]{:S(2)}) collective-permute-start(s16[272,512]{1,0:T(8,128)(2,1)S(1)} %get-tuple-element.37), channel_id=1, source_target_pairs={{0,2},{1,3},{2,4},{3,5},{4,6},{5,7},{6,0},{7,1},{8,10},{9,11},{10,... | collective-permute-start | bytes 835592 | tf_op jit(solution)/shard_map/ppermute | solution.py:271
  229.7 11.3 %collective-permute-start.22 = (s16[272,512]{1,0:T(8,128)(2,1)S(1)}, s16[272,512]{1,0:T(8,128)(2,1)S(1)}, u32[]{:S(2)}, u32[]{:S(2)}) collective-permute-start(s16[272,512]{1,0:T(8,128)(2,1)S(1)} %collective-permute-done.21), channel_id=1, source_target_pairs={{0,0},{1,1},{2,18},{3,19},{4,36},{5,37},{6,54},{7,55},{8,8},{9,9},... | collective-permute-start | bytes 835592 | tf_op jit(solution)/shard_map/ppermute | solution.py:272
  230.4 13.9 %collective-permute-start.24 = (s16[272,512]{1,0:T(8,128)(2,1)S(1)}, s16[272,512]{1,0:T(8,128)(2,1)S(1)}, u32[]{:S(2)}, u32[]{:S(2)}) collective-permute-start(s16[272,512]{1,0:T(8,128)(2,1)S(1)} %collective-permute-done.23), channel_id=1, source_target_pairs={{0,16},{1,17},{2,34},{3,35},{4,52},{5,53},{6,6},{7,7},{8,24},{9,25... | collective-permute-start | bytes 835592 | tf_op jit(solution)/shard_map/ppermute | solution.py:272
  239.1 12.2 %collective-permute-start.26 = (s16[272,512]{1,0:T(8,128)(2,1)S(1)}, s16[272,512]{1,0:T(8,128)(2,1)S(1)}, u32[]{:S(2)}, u32[]{:S(2)}) collective-permute-start(s16[272,512]{1,0:T(8,128)(2,1)S(1)} %collective-permute-done.25), channel_id=1, source_target_pairs={{0,32},{1,33},{2,50},{3,51},{4,4},{5,5},{6,22},{7,23},{8,40},{9,41... | collective-permute-start | bytes 835592 | tf_op jit(solution)/shard_map/ppermute | solution.py:272
  241.1 13.9 %collective-permute-start.32 = (s16[272,512]{1,0:T(8,128)(2,1)S(1)}, s16[272,512]{1,0:T(8,128)(2,1)S(1)}, u32[]{:S(2)}, u32[]{:S(2)}) collective-permute-start(s16[272,512]{1,0:T(8,128)(2,1)S(1)} %get-tuple-element.40), channel_id=1, source_target_pairs={{0,0},{1,1},{2,2},{3,3},{4,4},{5,5},{6,6},{7,7},{8,8},{9,9},{10,10... | collective-permute-start | bytes 835592 | tf_op jit(solution)/shard_map/ppermute | solution.py:271
  244.3 14.2 %collective-permute-start.34 = (s16[272,512]{1,0:T(8,128)(2,1)S(1)}, s16[272,512]{1,0:T(8,128)(2,1)S(1)}, u32[]{:S(2)}, u32[]{:S(2)}) collective-permute-start(s16[272,512]{1,0:T(8,128)(2,1)S(1)} %get-tuple-element.41), channel_id=1, source_target_pairs={{0,6},{1,7},{2,0},{3,1},{4,2},{5,3},{6,4},{7,5},{8,14},{9,15},{10,... | collective-permute-start | bytes 835592 | tf_op jit(solution)/shard_map/ppermute | solution.py:271
  251.3 20.7 %collective-permute-start.36 = (s16[272,512]{1,0:T(8,128)(2,1)S(1)}, s16[272,512]{1,0:T(8,128)(2,1)S(1)}, u32[]{:S(2)}, u32[]{:S(2)}) collective-permute-start(s16[272,512]{1,0:T(8,128)(2,1)S(1)} %get-tuple-element.42), channel_id=1, source_target_pairs={{0,4},{1,5},{2,6},{3,7},{4,0},{5,1},{6,2},{7,3},{8,12},{9,13},{10,... | collective-permute-start | bytes 835592 | tf_op jit(solution)/shard_map/ppermute | solution.py:271
  255.0 18.9 %collective-permute-start.28 = (s16[272,512]{1,0:T(8,128)(2,1)S(1)}, s16[272,512]{1,0:T(8,128)(2,1)S(1)}, u32[]{:S(2)}, u32[]{:S(2)}) collective-permute-start(s16[272,512]{1,0:T(8,128)(2,1)S(1)} %collective-permute-done.27), channel_id=1, source_target_pairs={{0,48},{1,49},{2,2},{3,3},{4,20},{5,21},{6,38},{7,39},{8,56},{9,57... | collective-permute-start | bytes 835592 | tf_op jit(solution)/shard_map/ppermute | solution.py:272
  258.5 16.2 %collective-permute-start.38 = (s16[272,512]{1,0:T(8,128)(2,1)S(1)}, s16[272,512]{1,0:T(8,128)(2,1)S(1)}, u32[]{:S(2)}, u32[]{:S(2)}) collective-permute-start(s16[272,512]{1,0:T(8,128)(2,1)S(1)} %get-tuple-element.43), channel_id=1, source_target_pairs={{0,2},{1,3},{2,4},{3,5},{4,6},{5,7},{6,0},{7,1},{8,10},{9,11},{10,... | collective-permute-start | bytes 835592 | tf_op jit(solution)/shard_map/ppermute | solution.py:271
  267.4 9.2 %collective-permute-start.33 = (s16[272,512]{1,0:T(8,128)(2,1)S(1)}, s16[272,512]{1,0:T(8,128)(2,1)S(1)}, u32[]{:S(2)}, u32[]{:S(2)}) collective-permute-start(s16[272,512]{1,0:T(8,128)(2,1)S(1)} %collective-permute-done.32), channel_id=1, source_target_pairs={{0,0},{1,1},{2,18},{3,19},{4,36},{5,37},{6,54},{7,55},{8,8},{9,9},... | collective-permute-start | bytes 835592 | tf_op jit(solution)/shard_map/ppermute | solution.py:272
  268.3 17.1 %collective-permute-start.35 = (s16[272,512]{1,0:T(8,128)(2,1)S(1)}, s16[272,512]{1,0:T(8,128)(2,1)S(1)}, u32[]{:S(2)}, u32[]{:S(2)}) collective-permute-start(s16[272,512]{1,0:T(8,128)(2,1)S(1)} %collective-permute-done.34), channel_id=1, source_target_pairs={{0,16},{1,17},{2,34},{3,35},{4,52},{5,53},{6,6},{7,7},{8,24},{9,25... | collective-permute-start | bytes 835592 | tf_op jit(solution)/shard_map/ppermute | solution.py:272
  272.1 16.6 %collective-permute-start.37 = (s16[272,512]{1,0:T(8,128)(2,1)S(1)}, s16[272,512]{1,0:T(8,128)(2,1)S(1)}, u32[]{:S(2)}, u32[]{:S(2)}) collective-permute-start(s16[272,512]{1,0:T(8,128)(2,1)S(1)} %collective-permute-done.36), channel_id=1, source_target_pairs={{0,32},{1,33},{2,50},{3,51},{4,4},{5,5},{6,22},{7,23},{8,40},{9,41... | collective-permute-start | bytes 835592 | tf_op jit(solution)/shard_map/ppermute | solution.py:272
  274.0 17.4 %collective-permute-start.43 = (s16[272,512]{1,0:T(8,128)(2,1)S(1)}, s16[272,512]{1,0:T(8,128)(2,1)S(1)}, u32[]{:S(2)}, u32[]{:S(2)}) collective-permute-start(s16[272,512]{1,0:T(8,128)(2,1)S(1)} %get-tuple-element.46), channel_id=1, source_target_pairs={{0,0},{1,1},{2,2},{3,3},{4,4},{5,5},{6,6},{7,7},{8,8},{9,9},{10,10... | collective-permute-start | bytes 835592 | tf_op jit(solution)/shard_map/ppermute | solution.py:271
  274.7 17.4 %collective-permute-start.45 = (s16[272,512]{1,0:T(8,128)(2,1)S(1)}, s16[272,512]{1,0:T(8,128)(2,1)S(1)}, u32[]{:S(2)}, u32[]{:S(2)}) collective-permute-start(s16[272,512]{1,0:T(8,128)(2,1)S(1)} %get-tuple-element.47), channel_id=1, source_target_pairs={{0,6},{1,7},{2,0},{3,1},{4,2},{5,3},{6,4},{7,5},{8,14},{9,15},{10,... | collective-permute-start | bytes 835592 | tf_op jit(solution)/shard_map/ppermute | solution.py:271
  276.6 19.9 %collective-permute-start.47 = (s16[272,512]{1,0:T(8,128)(2,1)S(1)}, s16[272,512]{1,0:T(8,128)(2,1)S(1)}, u32[]{:S(2)}, u32[]{:S(2)}) collective-permute-start(s16[272,512]{1,0:T(8,128)(2,1)S(1)} %get-tuple-element.48), channel_id=1, source_target_pairs={{0,4},{1,5},{2,6},{3,7},{4,0},{5,1},{6,2},{7,3},{8,12},{9,13},{10,... | collective-permute-start | bytes 835592 | tf_op jit(solution)/shard_map/ppermute | solution.py:271
  285.4 14.5 %collective-permute-start.49 = (s16[272,512]{1,0:T(8,128)(2,1)S(1)}, s16[272,512]{1,0:T(8,128)(2,1)S(1)}, u32[]{:S(2)}, u32[]{:S(2)}) collective-permute-start(s16[272,512]{1,0:T(8,128)(2,1)S(1)} %get-tuple-element.49), channel_id=1, source_target_pairs={{0,2},{1,3},{2,4},{3,5},{4,6},{5,7},{6,0},{7,1},{8,10},{9,11},{10,... | collective-permute-start | bytes 835592 | tf_op jit(solution)/shard_map/ppermute | solution.py:271
  288.6 14.7 %collective-permute-start.39 = (s16[272,512]{1,0:T(8,128)(2,1)S(1)}, s16[272,512]{1,0:T(8,128)(2,1)S(1)}, u32[]{:S(2)}, u32[]{:S(2)}) collective-permute-start(s16[272,512]{1,0:T(8,128)(2,1)S(1)} %collective-permute-done.38), channel_id=1, source_target_pairs={{0,48},{1,49},{2,2},{3,3},{4,20},{5,21},{6,38},{7,39},{8,56},{9,57... | collective-permute-start | bytes 835592 | tf_op jit(solution)/shard_map/ppermute | solution.py:272
  291.4 12.0 %collective-permute-start.44 = (s16[272,512]{1,0:T(8,128)(2,1)S(1)}, s16[272,512]{1,0:T(8,128)(2,1)S(1)}, u32[]{:S(2)}, u32[]{:S(2)}) collective-permute-start(s16[272,512]{1,0:T(8,128)(2,1)S(1)} %collective-permute-done.43), channel_id=1, source_target_pairs={{0,0},{1,1},{2,18},{3,19},{4,36},{5,37},{6,54},{7,55},{8,8},{9,9},... | collective-permute-start | bytes 835592 | tf_op jit(solution)/shard_map/ppermute | solution.py:272
  292.1 12.1 %collective-permute-start.46 = (s16[272,512]{1,0:T(8,128)(2,1)S(1)}, s16[272,512]{1,0:T(8,128)(2,1)S(1)}, u32[]{:S(2)}, u32[]{:S(2)}) collective-permute-start(s16[272,512]{1,0:T(8,128)(2,1)S(1)} %collective-permute-done.45), channel_id=1, source_target_pairs={{0,16},{1,17},{2,34},{3,35},{4,52},{5,53},{6,6},{7,7},{8,24},{9,25... | collective-permute-start | bytes 835592 | tf_op jit(solution)/shard_map/ppermute | solution.py:272
  296.6 13.9 %collective-permute-start.48 = (s16[272,512]{1,0:T(8,128)(2,1)S(1)}, s16[272,512]{1,0:T(8,128)(2,1)S(1)}, u32[]{:S(2)}, u32[]{:S(2)}) collective-permute-start(s16[272,512]{1,0:T(8,128)(2,1)S(1)} %collective-permute-done.47), channel_id=1, source_target_pairs={{0,32},{1,33},{2,50},{3,51},{4,4},{5,5},{6,22},{7,23},{8,40},{9,41... | collective-permute-start | bytes 835592 | tf_op jit(solution)/shard_map/ppermute | solution.py:272
  299.9 12.1 %collective-permute-start.50 = (s16[272,512]{1,0:T(8,128)(2,1)S(1)}, s16[272,512]{1,0:T(8,128)(2,1)S(1)}, u32[]{:S(2)}, u32[]{:S(2)}) collective-permute-start(s16[272,512]{1,0:T(8,128)(2,1)S(1)} %collective-permute-done.49), channel_id=1, source_target_pairs={{0,48},{1,49},{2,2},{3,3},{4,20},{5,21},{6,38},{7,39},{8,56},{9,57... | collective-permute-start | bytes 835592 | tf_op jit(solution)/shard_map/ppermute | solution.py:272
  (5 other events, 102.3 us)

commit v2 on v0

v2 whole, which is shorter than its diff:
```python
import jax
import jax.numpy as jnp
from jax import lax
from jax.experimental import pallas as pl
from jax.experimental.pallas import tpu as pltpu
from jax.sharding import PartitionSpec as P

BLOCK = 128
EPSILON = 1e-6
AXES = ("ckpt", "row")
OWN, PARTNER, KEEP, YHI, SLOT, CORE = range(6)
TILE = 512
ROWS = 1024
CHUNK = 256
CHUNKS = ROWS // CHUNK
BANDS = CHUNK // BLOCK
BITS = CHUNK // 16
LAST = CHUNKS - 1
UNITS = 16


def device_index(x, y, z, core):
    y_hi, y_lo = divmod(y, 2)
    return (y_hi * 4 + x) * 16 + y_lo * 8 + z * 2 + core


def permutation(target):
    return [
        (device_index(x, y, z, core), device_index(*target(x, y, z, core)))
        for x in range(4)
        for y in range(4)
        for z in range(4)
        for core in range(2)
    ]


def pair_of(x, y, z, core):
    return (x + 1 - 2 * ((x + core) % 2)) % 4, y, z, core


def z_target(m, x, y, z, core):
    away = (z - x) % 4
    return x, y, (x + core) % 2 + 2 * (m ^ (away // 2)), away % 2


def x_target(m, x, y, z, core):
    return (x + core + 2 * (m ^ (z // 2))) % 4, y, z, (z - x) % 2


ACROSS = {0: 1, 1: 3, 2: 0, 3: 2}
BESIDE = {0: 0, 1: 2, 2: 1, 3: 3}
PAIR_PERM = permutation(pair_of)
ACROSS_PERM = permutation(lambda x, y, z, core: (x, ACROSS[y], z, core))
BESIDE_PERM = permutation(lambda x, y, z, core: (x, BESIDE[y], z, core))
Z_PERMS = [permutation(lambda *at, m=m: z_target(m, *at)) for m in range(2)]
X_PERMS = [permutation(lambda *at, m=m: x_target(m, *at)) for m in range(2)]
CORE_PERM = permutation(lambda x, y, z, core: (x, y, z, 1 - core))


def call(kernel, grid, scalars, inputs, outputs, after=(), scratch=(), aliases=None):
    first = len(scalars) + len(inputs)

    def whole(*refs):
        kernel(*refs[:first], *refs[first + len(after) :])

    moved = sum(a.dtype.itemsize * a.size for a, _ in inputs)
    return pl.pallas_call(
        whole,
        grid_spec=pltpu.PrefetchScalarGridSpec(
            num_scalar_prefetch=len(scalars),
            grid=grid,
            in_specs=[spec for _, spec in inputs] + [pl.BlockSpec(memory_space=pl.ANY)] * len(after),
            out_specs=[spec for _, _, spec in outputs],
            scratch_shapes=scratch,
        ),
        out_shape=[jax.ShapeDtypeStruct(s, d) for s, d, _ in outputs],
        input_output_aliases=aliases or {},
        compiler_params=pltpu.CompilerParams(vmem_limit_bytes=40 * 1024 * 1024),
        cost_estimate=pl.CostEstimate(flops=0, bytes_accessed=moved, transcendentals=0),
    )(*scalars, *[a for a, _ in inputs], *after)


def later(values, *after):
    return lax.optimization_barrier((tuple(values), after))[0] if after else values


ANYWHERE = pl.BlockSpec(memory_space=pl.ANY)


def pack(chunk, place, codes, wide_exps, after):
    extra = UNITS if chunk == 0 else 0

    def kernel(place, codes, wide_exps, sent, sems):
        copies = []
        for group in range(4):
            y_lo, t = divmod(group, 2)
            first = pl.multiple_of((y_lo * 4 + 1 - place[KEEP] + 2 * t) * 2 * TILE, BLOCK)
            cols, to = pl.ds(first, 2 * TILE), pl.ds(group * 2 * TILE, 2 * TILE)
            copies.append(
                pltpu.make_async_copy(
                    codes.at[0, pl.ds(chunk * CHUNK, CHUNK), cols],
                    sent.at[pl.ds(0, CHUNK), to],
                    sems.at[group],
                )
            )
            if extra:
                copies.append(
                    pltpu.make_async_copy(
                        wide_exps.at[:, cols], sent.at[pl.ds(CHUNK, UNITS), to], sems.at[4 + group]
                    )
                )
        for copy in copies:
            copy.start()
        for copy in copies:
            copy.wait()

    return call(
        kernel,
        (),
        [place],
        [(codes, ANYWHERE), (wide_exps, ANYWHERE)],
        [((CHUNK + extra, 8 * TILE), jnp.bfloat16, ANYWHERE)],
        after,
        [pltpu.SemaphoreType.DMA((8,))],
    )[0]


def whole_number(ref):
    return ref[...].astype(jnp.float32).astype(jnp.int32)


def add_pairs(chunk, place, weights, wide_exps, codes, first_received, received, after):
    extra = UNITS if chunk == 0 else 0

    def kernel(place, weights, *refs):
        own_weight, partner_weight = weights[place[OWN]], weights[place[PARTNER]]
        for at in range(2):
            kept, came, own, partner, out = refs[at::2]
            own, partner = whole_number(own), whole_number(partner)
            unit = jnp.minimum(own, partner)
            own = (jnp.full(own.shape, own_weight, jnp.int32) << (own - unit)).astype(jnp.float32)
            partner = (jnp.full(own.shape, partner_weight, jnp.int32) << (partner - unit)).astype(
                jnp.float32
            )
            for band in range(BANDS):
                row = chunk * BANDS + band
                rows = pl.ds(band * BLOCK, BLOCK)
                for col in range(TILE // BLOCK):
                    cols = slice(col * BLOCK, (col + 1) * BLOCK)
                    total = (
                        kept[0, rows, cols].astype(jnp.float32) * own[row : row + 1, cols]
                        + came[rows, cols].astype(jnp.float32) * partner[row : row + 1, cols]
                    )
                    out[rows, cols] = total.astype(jnp.int32).astype(jnp.int16)
            if extra:
                out[pl.ds(CHUNK, UNITS), :] = unit.astype(jnp.int16)

    def kept_col(y_lo, t):
        return lambda p: 2 * (y_lo(p) * 4 + p[KEEP] + 2 * (t // 2)) + t % 2

    far, near = (lambda p: 1 - p[YHI]), (lambda p: p[YHI])

    def kept_at(y_lo, row):
        return lambda t, p, w: (*row, 2 * (y_lo(p) * 4 + p[KEEP] + 2 * (t // 2)) + t % 2)

    def came_at(y_lo, row):
        return lambda t, p, w: (row, y_lo(p) * 4 + t)

    sent = (CHUNK + extra, TILE)
    return call(
        kernel,
        (4,),
        [place, weights],
        [(codes, pl.BlockSpec((1, CHUNK, TILE), kept_at(y, (0, chunk)))) for y in (far, near)]
        + [(received, pl.BlockSpec((CHUNK, TILE), came_at(y, 0))) for y in (far, near)]
        + [(wide_exps, pl.BlockSpec((UNITS, TILE), kept_at(y, (0,)))) for y in (far, near)]
        + [(first_received, pl.BlockSpec((UNITS, TILE), came_at(y, CHUNK // UNITS))) for y in (far, near)],
        [((CHUNK + extra, 4 * TILE), jnp.int16, pl.BlockSpec(sent, lambda t, *_: (0, t)))] * 2,
        after,
    )


def add_fours(chunk, place, first_far, first_near, far, near, after):
    extra = UNITS if chunk == 0 else 0

    def kernel(place, far, near, far_unit, near_unit, *outs):
        far_unit, near_unit = far_unit[...].astype(jnp.int32), near_unit[...].astype(jnp.int32)
        unit = jnp.minimum(far_unit, near_unit)
        far_unit, near_unit = far_unit - unit, near_unit - unit

        def fill(out):
            for col in range(2 * TILE // BLOCK):
                cols = slice(col * BLOCK, (col + 1) * BLOCK)
                odds = []
                for band in range(BANDS):
                    row = chunk * BANDS + band
                    rows = pl.ds(band * BLOCK, BLOCK)
                    total = (
                        far[rows, cols].astype(jnp.int32)
                        << jnp.broadcast_to(far_unit[row : row + 1, cols], (BLOCK, BLOCK))
                    ) + (
                        near[rows, cols].astype(jnp.int32)
                        << jnp.broadcast_to(near_unit[row : row + 1, cols], (BLOCK, BLOCK))
                    )
                    out[rows, cols] = (total >> 1).astype(jnp.int16)
                    odd = total & 1
                    packed = odd[0:8]
                    for group in range(1, 16):
                        packed = packed | (odd[8 * group : 8 * group + 8] << group)
                    odds.append(packed)
                out[pl.ds(CHUNK, BITS), cols] = jnp.concatenate(odds, axis=0).astype(jnp.int16)
            if extra:
                out[pl.ds(CHUNK + BITS, UNITS), :] = unit.astype(jnp.int16)

        for slot, out in enumerate(outs):
            pl.when(pl.program_id(0) == slot)(lambda out=out: fill(out))

    rows = CHUNK + BITS + extra
    picked = lambda t, p: jnp.bitwise_xor(t, p[SLOT])
    block = pl.BlockSpec((CHUNK, 2 * TILE), lambda t, p: (0, picked(t, p)))
    units = pl.BlockSpec((UNITS, 2 * TILE), lambda t, p: (CHUNK // UNITS, picked(t, p)))
    return call(
        kernel,
        (2,),
        [place],
        [(far, block), (near, block), (first_far, units), (first_near, units)],
        [((rows, 2 * TILE), jnp.int16, pl.BlockSpec((rows, 2 * TILE), lambda t, p: (0, 0)))] * 2,
        after,
    )


def finish(chunk, place, denominator, first_parts, parts, before):
    chunks, row0 = (1, 0) if chunk == LAST else (CHUNKS - 1, chunk)
    per_half = BANDS * (TILE // BLOCK)

    def kernel(place, denominator, *refs):
        parts, units = refs[:2], refs[2:4]
        old_scales = refs[4] if before else None
        mine, other, scales, summed, factors = refs[-5:]
        core = place[CORE]
        divisor = jnp.full((1, 1), denominator[0], jnp.int32).astype(jnp.float32)
        units = [
            (1 << (unit[...].astype(jnp.int32) + 8)).astype(jnp.float32) * (1.0 / 256) for unit in units
        ]

        def fours(ref, unit, band, cols):
            packed = ref[pl.ds(CHUNK, BITS), cols].astype(jnp.int32)[8 * band : 8 * band + 8]
            odd = jnp.concatenate([(packed >> group) & 1 for group in range(16)], axis=0)
            total = (ref[pl.ds(band * BLOCK, BLOCK), cols].astype(jnp.int32) << 1) + odd
            row = chunk * BANDS + band
            return total.astype(jnp.float32) * unit[row : row + 1, cols]

        blocks = [(h, band, col) for h in range(2) for band in range(BANDS) for col in range(TILE // BLOCK)]
        tops = []
        for half, band, col in blocks:
            cols = slice(half * TILE + col * BLOCK, half * TILE + (col + 1) * BLOCK)
            total = fours(parts[0], units[0], band, cols) + fours(parts[1], units[1], band, cols)
            summed[half, pl.ds(band * BLOCK, BLOCK), col * BLOCK : (col + 1) * BLOCK] = total
            tops.append(jnp.max(jnp.abs(total), axis=0, keepdims=True))
        scale = jnp.max(jnp.concatenate(tops, axis=0), axis=1, keepdims=True) / divisor
        factors[...] = jnp.broadcast_to(1.0 / (divisor * (scale + EPSILON)), factors.shape)
        found = old_scales[...] if before else jnp.zeros_like(scales)
        row_at = lax.broadcasted_iota(jnp.int32, scales.shape, 0)
        col_at = lax.broadcasted_iota(jnp.int32, scales.shape, 1)
        for at, (half, band, col) in enumerate(blocks):
            here = (row_at == chunk * BANDS + band) & (col_at == half * (TILE // BLOCK) + col)
            found = jnp.where(here, scale[at : at + 1, :], found)
        scales[...] = found
        for half, out in ((core, mine), (1 - core, other)):
            for at in range(per_half):
                band, col = divmod(at, TILE // BLOCK)
                rows, cols = pl.ds(band * BLOCK, BLOCK), slice(col * BLOCK, (col + 1) * BLOCK)
                factor = factors[pl.ds(half * per_half + at, 1), :]
                out[rows, cols] = (summed[half, rows, cols] * factor).astype(jnp.bfloat16)

    small = pl.BlockSpec((8, 8), lambda t, *_: (0, 0))
    units = pl.BlockSpec((UNITS, 2 * TILE), lambda t, *_: ((CHUNK + BITS) // UNITS, 0))
    inputs = [(part, pl.BlockSpec((CHUNK + BITS, 2 * TILE), lambda t, *_: (0, 0))) for part in parts]
    inputs += [(part, units) for part in first_parts]
    after, aliases = (), {}
    if before:
        tiles, other, scales = before
        inputs.append((scales, small))
        after, aliases = (tiles,), {7: 0}
        if chunk != LAST:
            after, aliases = (tiles, other), {7: 0, 8: 1}
    tile = (CHUNK, TILE)
    return call(
        kernel,
        (1,),
        [place, denominator],
        inputs,
        [
            ((2 * ROWS, TILE), jnp.bfloat16, pl.BlockSpec(tile, lambda t, p, d: (p[CORE] * CHUNKS + chunk, 0))),
            ((chunks * CHUNK, TILE), jnp.bfloat16, pl.BlockSpec(tile, lambda t, *_: (row0, 0))),
            ((8, 8), jnp.float32, small),
        ],
        after,
        [pltpu.VMEM((2, CHUNK, TILE), jnp.float32), pltpu.VMEM((2 * per_half, BLOCK), jnp.float32)],
        aliases,
    )


def assemble(place, tiles, came, scales, scales_came):
    def kernel(place, tiles_in, came, last_came, scales, scales_came, tiles, all_scales, sems):
        core = place[CORE]
        copies, first = [], 0
        for at, part in enumerate((came, last_came)):
            rows = pl.ds(pl.multiple_of((1 - core) * ROWS + first, CHUNK), part.shape[0])
            copies.append(pltpu.make_async_copy(part, tiles.at[rows, :], sems.at[at]))
            first += part.shape[0]
        for copy in copies:
            copy.start()
        for mine in range(2):

            @pl.when(core == mine)
            def _():
                cols = slice(4 * mine, 4 * mine + 4)
                all_scales[8 * mine : 8 * mine + 8, :] = scales[:, cols]
                all_scales[8 - 8 * mine : 16 - 8 * mine, :] = scales_came[:, cols]

        for copy in copies:
            copy.wait()

    vmem = pl.BlockSpec(memory_space=pltpu.VMEM)
    return call(
        kernel,
        (),
        [place],
        [(tiles, ANYWHERE), *[(part, ANYWHERE) for part in came], (scales, vmem), (scales_came, vmem)],
        [((2 * ROWS, TILE), jnp.bfloat16, ANYWHERE), ((16, 4), jnp.float32, vmem)],
        (),
        [pltpu.SemaphoreType.DMA((2,))],
        {1: 0},
    )


def body(quant_codes, exponents, numerators, denominator):
    y_hi, x = jnp.divmod(lax.axis_index("ckpt"), 4)
    row = lax.axis_index("row")
    z, core = (row // 2) % 4, row % 2
    keep = (x + core) % 2
    place = jnp.stack(
        [y_hi * 4 + x, y_hi * 4 + (x + 1 - 2 * keep) % 4, keep, y_hi, ((z - x) % 4) // 2, core]
    ).astype(jnp.int32)
    wide_exps = jnp.pad(jnp.repeat(exponents[0], BLOCK, axis=1), ((0, UNITS - 8), (0, 0))).astype(
        jnp.bfloat16
    )

    def swap_pairs(chunk, after):
        return lax.ppermute(pack(chunk, place, quant_codes, wide_exps, after), AXES, PAIR_PERM)

    def pairs_of(chunk, after):
        return add_pairs(
            chunk, place, numerators, wide_exps, quant_codes, received[0], received[chunk], after
        )

    def move_y(pair, *after):
        far, near = later(pair, *after)
        return lax.ppermute(far, AXES, ACROSS_PERM), lax.ppermute(near, AXES, BESIDE_PERM)

    def fours_of(chunk, after):
        return add_fours(chunk, place, *moved[0], *moved[chunk], after)

    def move(pair, perms, *after):
        return [lax.ppermute(part, AXES, perm) for part, perm in zip(later(pair, *after), perms)]

    def finished(chunk, before):
        return finish(chunk, place, denominator, parts[0], parts[chunk], before)

    received, pairs, moved, fours, parts = {}, {}, {}, {}, {}
    received[0] = swap_pairs(0, ())
    received[1] = swap_pairs(1, ())
    pairs[0] = pairs_of(0, ())
    moved[0] = move_y(pairs[0])
    received[2] = swap_pairs(2, pairs[0])
    pairs[1] = pairs_of(1, pairs[0])
    fours[0] = fours_of(0, pairs[1])
    moved[1] = move_y(pairs[1], fours[0])
    received[3] = swap_pairs(3, (*pairs[1], *fours[0]))
    parts[0] = move(fours[0], Z_PERMS)
    pairs[2] = pairs_of(2, (*pairs[1], *fours[0]))
    fours[1] = fours_of(1, pairs[2])
    moved[2] = move_y(pairs[2], fours[1])
    parts[1] = move(fours[1], Z_PERMS, parts[0])
    pairs[3] = pairs_of(3, (*fours[1], *parts[0]))
    parts[0] = move(parts[0], X_PERMS, received[3])
    fours[2] = fours_of(2, pairs[3])
    moved[3] = move_y(pairs[3], fours[2])
    parts[2] = move(fours[2], Z_PERMS, parts[1])
    parts[1] = move(parts[1], X_PERMS, parts[0])
    done = finished(0, None)
    done = finished(1, done)
    fours[3] = fours_of(3, tuple(done))
    parts[3] = move(fours[3], Z_PERMS, parts[2])
    parts[2] = move(parts[2], X_PERMS, parts[1])
    parts[3] = move(parts[3], X_PERMS)
    done = finished(2, done)
    came = lax.ppermute(done[1], AXES, CORE_PERM)
    tiles, other, scales = finished(3, done)
    last_came = lax.ppermute(other, AXES, CORE_PERM)
    scales_came = lax.ppermute(scales, AXES, CORE_PERM)
    return tuple(assemble(place, tiles, (came, last_came), scales, scales_came))


def solution(mesh):
    placed = (P("ckpt", "row", None), P("ckpt", "row", None), P(), P())
    return jax.shard_map(
        body,
        mesh=mesh,
        in_specs=placed,
        out_specs=(P("ckpt", "row"), P("ckpt", "row")),
        check_vma=False,
    )
```

time: 896 us -> 208 us (0.23)
  blocking collectives: 372 us -> 0 us
  waiting for transfers between devices: 358 us -> 80 us
  local copies, waits for them, and re-layouts: 104 us -> 2.59 us
  starting transfers between devices: 0.04 us -> 80.5 us
  other arithmetic: 44.1 us -> 0.69 us
  Pallas kernels: 0 us -> 40.2 us
  between operations: 15.4 us -> 1.79 us
    all_to_all x1 -> x0, blocking collectives: 372 us -> none  [body(): lax.all_to_all(partial_rows, 'row', split_axis=1, concat_axis=0, tiled=True)]
    reduce_scatter x1 -> x0, waiting for transfers between devices: 358 us -> none  [body(): summed = lax.psum_scatter(relaid, 'ckpt', scatter_dimension=0, tiled=True)]
    ppermute x0 -> x31, starting transfers between devices: none -> 80.5 us  [the longest x16 50.7 us: move(): lax.ppermute(part, AXES, perm)]
    ppermute x0 -> x31, waiting for transfers between devices: none -> 80 us  [the longest x4 38.5 us: swap_pairs(): lax.ppermute(pack(chunk, place, quant_codes, wide_exps, after), AXES, PAI...]
    mul x3 -> x0, local copies, waits for them, and re-layouts: 75.3 us -> none  [the longest x2 47.1 us: weigh_codes(): scaled = grid_values * powers_block[:, :, None, :, None]]
    pallas_call x0 -> x17, Pallas kernels: none -> 40.2 us  [call(): pl.pallas_call(whole, grid_spec=pltpu.PrefetchScalarGridSpec(num_scalar_p...]
    mul x2 -> x0, other arithmetic: 34.3 us -> none  [the longest x1 33.6 us: weigh_codes(): weighted = jnp.sum(own_weights[:, None, None, None, None] * scaled, axis=0)]
    unnamed x4, local copies, waits for them, and re-layouts: 21.8 us -> 1.6 us
  transfers between devices with their start and end apart: 1 -> 31, of which waited for: 1 -> 13; matrix products, arithmetic and copies ran while one was open for 0% -> 0% of each run, Pallas kernels for 0% -> 18%
where the time goes in v2:
time: 208 us; the launch traced here: 206 us
  starting transfers between devices  80.5 us (39%)
  waiting for transfers between devices  80 us (38%)
  Pallas kernels  40.2 us (19%)
  local copies, waits for them, and re-layouts  2.59 us (1%)
    ppermute x16, starting transfers between devices, move(): lax.ppermute(part, AXES, perm)  50.7 us
    pallas_call x17, Pallas kernels, call(): pl.pallas_call(whole, grid_spec=pltpu.PrefetchScalarGridSpec(num_scalar_p...  40.2 us
    ppermute x4, waiting for transfers between devices, swap_pairs(): lax.ppermute(pack(chunk, place, quant_codes, wide_exps, after), AXES, PAI...  38.5 us
    ppermute x16, waiting for transfers between devices, move(): lax.ppermute(part, AXES, perm)  21.9 us
    ppermute x4, waiting for transfers between devices, move_y(): lax.ppermute(far, AXES, ACROSS_PERM)  18.5 us
    ppermute x4, starting transfers between devices, move_y(): lax.ppermute(far, AXES, ACROSS_PERM)  11.1 us
    ppermute x1, starting transfers between devices, body(): came = lax.ppermute(done[1], AXES, CORE_PERM)  6.2 us
    ppermute x1, starting transfers between devices, body(): last_came = lax.ppermute(other, AXES, CORE_PERM)  5.16 us
  transfers between devices with their start and end apart: 31, of which 13 were waited for; matrix products, arithmetic and copies ran while one was open for 0% of the time, Pallas kernels for 18%

profile of v2, /device:TPU:0, one launch (start us, length us, event | category | flops | bytes accessed | tf_op | source)
XLA Modules:
  0.0 205.7 jit_solution(18122563370757748720)
XLA Ops:
  1.8 2.2 %shard_map.60 = bf16[272,4096]{1,0:T(8,128)(2,1)S(1)} custom-call(s32[6]{0:T(128)S(1)} %stack.27.refs_0_, bf16[1,1024,8192]{2,1,0:T(8,128)(2,1)} %refs_3_.7, bf16[16,8192]{1,0:T(8,128)(2,1)S(1)} %pad.5.refs_2_.refs_6_.refs_7_), custom_call_target="tpu_custom_call" | custom-call | bytes 17039360 | tf_op jit(solution)/shard_map/pallas_call | solution.py:67
  4.0 1.7 collective-permute-start.1
  5.6 2.1 %shard_map.59 = bf16[256,4096]{1,0:T(8,128)(2,1)S(1)} custom-call(s32[6]{0:T(128)S(1)} %stack.27.refs_0_, bf16[1,1024,8192]{2,1,0:T(8,128)(2,1)} %refs_3_.7, bf16[16,8192]{1,0:T(8,128)(2,1)S(1)} %pad.5.refs_2_.refs_6_.refs_7_), custom_call_target="tpu_custom_call" | custom-call | bytes 17039360 | tf_op jit(solution)/shard_map/pallas_call | solution.py:67
  8.3 23.2 %collective-permute-done.1.refs_4_.refs_5_.refs_8_.refs_9_ = bf16[272,4096]{1,0:T(8,128)(2,1)S(1)} collective-permute-done((bf16[272,4096]{1,0:T(8,128)(2,1)S(1)}, bf16[272,4096]{1,0:T(8,128)(2,1)S(1)}, u32[]{:S(2)}, u32[]{:S(2)}) %collective-permute-start.1) | collective-permute-done | bytes 2228256 | tf_op jit(solution)/shard_map/ppermute | solution.py:351
  31.5 4.1 %shard_map.61 = (s16[272,2048]{1,0:T(8,128)(2,1)S(1)}, s16[272,2048]{1,0:T(8,128)(2,1)S(1)}) custom-call(s32[6]{0:T(128)S(1)} %stack.27.refs_0_, s32[8]{0:T(128)S(1)} %copy-done.1, bf16[1,1024,8192]{2,1,0:T(8,128)(2,1)} %refs_3_.7, bf16[1,1024,8192]{2,1,0:T(8,128)(2,1)} %refs_3_.7, ...), custom_call_target="tpu_custom_call" | custom-call | bytes 42991616 | tf_op jit(solution)/shard_map/pallas_call | solution.py:67
  35.6 1.7 collective-permute-start.2
  37.3 0.7 collective-permute-start.3
  38.0 2.1 %shard_map.65 = bf16[256,4096]{1,0:T(8,128)(2,1)S(1)} custom-call(s32[6]{0:T(128)S(1)} %stack.27.refs_0_, bf16[1,1024,8192]{2,1,0:T(8,128)(2,1)} %refs_3_.7, bf16[16,8192]{1,0:T(8,128)(2,1)S(1)} %pad.5.refs_2_.refs_6_.refs_7_, s16[272,2048]{1,0:T(8,128)(2,1)S(1)} %get-tuple-element.48.refs_10_.refs_3_, s16[272,2048]{1,0:T(8,128)(2,1)S(1)} %get-tuple-element.49.refs_11_.refs_4_), custom_call_target="tpu_custom_call" | custom-call | bytes 17039360 | tf_op jit(solution)/shard_map/pallas_call | solution.py:67
  40.2 1.6 collective-permute-start.7
  41.8 12.2 %collective-permute-done.refs_4_.refs_5_ = bf16[256,4096]{1,0:T(8,128)(2,1)S(1)} collective-permute-done((bf16[256,4096]{1,0:T(8,128)(2,1)S(1)}, bf16[256,4096]{1,0:T(8,128)(2,1)S(1)}, u32[]{:S(2)}, u32[]{:S(2)}) %collective-permute-start) | collective-permute-done | bytes 2097184 | tf_op jit(solution)/shard_map/ppermute | solution.py:351
  54.0 4.0 %shard_map.62 = (s16[256,2048]{1,0:T(8,128)(2,1)S(1)}, s16[256,2048]{1,0:T(8,128)(2,1)S(1)}) custom-call(s32[6]{0:T(128)S(1)} %stack.27.refs_0_, s32[8]{0:T(128)S(1)} %copy-done.1, bf16[1,1024,8192]{2,1,0:T(8,128)(2,1)} %refs_3_.7, bf16[1,1024,8192]{2,1,0:T(8,128)(2,1)} %refs_3_.7, bf16[256,4096]{1,0:T(8,128)(2,1)S(1)} %collective-permute-done.refs_4_.refs_5_, ...), custom_call_target="tpu_custom_call" | custom-call | bytes 42729472 | tf_op jit(solution)/shard_map/pallas_call | solution.py:67
  58.0 5.5 %collective-permute-done.2.refs_1_.refs_3_ = s16[272,2048]{1,0:T(8,128)(2,1)S(1)} collective-permute-done((s16[272,2048]{1,0:T(8,128)(2,1)S(1)}, s16[272,2048]{1,0:T(8,128)(2,1)S(1)}, u32[]{:S(2)}, u32[]{:S(2)}) %collective-permute-start.2) | collective-permute-done | bytes 1114144 | tf_op jit(solution)/shard_map/ppermute | solution.py:360
  63.6 1.6 shard_map.63
  65.1 2.1 %shard_map.64 = bf16[256,4096]{1,0:T(8,128)(2,1)S(1)} custom-call(s32[6]{0:T(128)S(1)} %stack.27.refs_0_, bf16[1,1024,8192]{2,1,0:T(8,128)(2,1)} %refs_3_.7, bf16[16,8192]{1,0:T(8,128)(2,1)S(1)} %pad.5.refs_2_.refs_6_.refs_7_, s16[256,2048]{1,0:T(8,128)(2,1)S(1)} %get-tuple-element.54.refs_5_.refs_3_.refs_10_, ...), custom_call_target="tpu_custom_call" | custom-call | bytes 17039360 | tf_op jit(solution)/shard_map/pallas_call | solution.py:67
  68.0 4.0 %collective-permute-start.5 = (s16[256,2048]{1,0:T(8,128)(2,1)S(1)}, s16[256,2048]{1,0:T(8,128)(2,1)S(1)}, u32[]{:S(2)}, u32[]{:S(2)}) collective-permute-start(s16[256,2048]{1,0:T(8,128)(2,1)S(1)} %get-tuple-element.54.refs_5_.refs_3_.refs_10_), channel_id=1, source_target_pairs={{0,8},{1,9},{2,10},{3,11},{4,12},{5,13},{6,14},{7,15},{8,72},{9,73... | collective-permute-start | bytes 3145736 | tf_op jit(solution)/shard_map/ppermute | solution.py:360
  73.4 3.1 %collective-permute-done.7.refs_4_.refs_5_ = bf16[256,4096]{1,0:T(8,128)(2,1)S(1)} collective-permute-done((bf16[256,4096]{1,0:T(8,128)(2,1)S(1)}, bf16[256,4096]{1,0:T(8,128)(2,1)S(1)}, u32[]{:S(2)}, u32[]{:S(2)}) %collective-permute-start.7) | collective-permute-done | bytes 2097184 | tf_op jit(solution)/shard_map/ppermute | solution.py:351
  76.4 5.9 %collective-permute-start.9 = (s16[288,1024]{1,0:T(8,128)(2,1)S(1)}, s16[288,1024]{1,0:T(8,128)(2,1)S(1)}, u32[]{:S(2)}, u32[]{:S(2)}) collective-permute-start(s16[288,1024]{1,0:T(8,128)(2,1)S(1)} %get-tuple-element.53.refs_6_.refs_13_), channel_id=1, source_target_pairs={{0,4},{1,6},{2,5},{3,7},{4,0},{5,2},{6,1},{7,3},{8,12},{9,14},{10,... | collective-permute-start | bytes 1769480 | tf_op jit(solution)/shard_map/ppermute | solution.py:366
  82.3 4.1 %shard_map.66 = (s16[256,2048]{1,0:T(8,128)(2,1)S(1)}, s16[256,2048]{1,0:T(8,128)(2,1)S(1)}) custom-call(s32[6]{0:T(128)S(1)} %stack.27.refs_0_, s32[8]{0:T(128)S(1)} %copy-done.1, bf16[1,1024,8192]{2,1,0:T(8,128)(2,1)} %refs_3_.7, bf16[1,1024,8192]{2,1,0:T(8,128)(2,1)} %refs_3_.7, bf16[256,4096]{1,0:T(8,128)(2,1)S(1)} %collective-permute-done.7.refs_4_.refs_5_, ...), custom_call_target="tpu_custom_call" | custom-call | bytes 42729472 | tf_op jit(solution)/shard_map/pallas_call | solution.py:67
  86.4 9.7 %collective-permute-done.5.refs_1_ = s16[256,2048]{1,0:T(8,128)(2,1)S(1)} collective-permute-done((s16[256,2048]{1,0:T(8,128)(2,1)S(1)}, s16[256,2048]{1,0:T(8,128)(2,1)S(1)}, u32[]{:S(2)}, u32[]{:S(2)}) %collective-permute-start.5) | collective-permute-done | bytes 1048608 | tf_op jit(solution)/shard_map/ppermute | solution.py:360
  96.0 1.5 shard_map.67
  98.3 3.5 %collective-permute-start.10 = (s16[256,2048]{1,0:T(8,128)(2,1)S(1)}, s16[256,2048]{1,0:T(8,128)(2,1)S(1)}, u32[]{:S(2)}, u32[]{:S(2)}) collective-permute-start(s16[256,2048]{1,0:T(8,128)(2,1)S(1)} %get-tuple-element.62.refs_5_), channel_id=1, source_target_pairs={{0,8},{1,9},{2,10},{3,11},{4,12},{5,13},{6,14},{7,15},{8,72},{9,73... | collective-permute-start | bytes 3145736 | tf_op jit(solution)/shard_map/ppermute | solution.py:360
  101.8 0.7 collective-permute-start.11
  103.3 5.9 %collective-permute-start.17 = (s16[288,1024]{1,0:T(8,128)(2,1)S(1)}, s16[288,1024]{1,0:T(8,128)(2,1)S(1)}, u32[]{:S(2)}, u32[]{:S(2)}) collective-permute-start(s16[288,1024]{1,0:T(8,128)(2,1)S(1)} %collective-permute-done.9.refs_13_), channel_id=1, source_target_pairs={{0,32},{1,48},{2,35},{3,51},{4,4},{5,20},{6,7},{7,23},{8,40},{9,56... | collective-permute-start | bytes 1769480 | tf_op jit(solution)/shard_map/ppermute | solution.py:366
  109.2 1.9 collective-permute-start.15
  111.2 11.1 %collective-permute-done.15 = s16[272,1024]{1,0:T(8,128)(2,1)S(1)} collective-permute-done((s16[272,1024]{1,0:T(8,128)(2,1)S(1)}, s16[272,1024]{1,0:T(8,128)(2,1)S(1)}, u32[]{:S(2)}, u32[]{:S(2)}) %collective-permute-start.15) | collective-permute-done | bytes 557088 | tf_op jit(solution)/shard_map/ppermute | solution.py:366
  123.0 4.1 %shard_map.68 = (s16[256,2048]{1,0:T(8,128)(2,1)S(1)}, s16[256,2048]{1,0:T(8,128)(2,1)S(1)}) custom-call(s32[6]{0:T(128)S(1)} %stack.27.refs_0_, s32[8]{0:T(128)S(1)} %copy-done.1, bf16[1,1024,8192]{2,1,0:T(8,128)(2,1)} %refs_3_.7, bf16[1,1024,8192]{2,1,0:T(8,128)(2,1)} %refs_3_.7, bf16[256,4096]{1,0:T(8,128)(2,1)S(1)} %collective-permute-done.4.refs_4_.refs_5_, ...), custom_call_target="tpu_custom_call" | custom-call | bytes 42729472 | tf_op jit(solution)/shard_map/pallas_call | solution.py:67
  127.1 1.5 shard_map.69
  128.6 1.8 collective-permute-start.12
  131.2 6.2 %collective-permute-start.19 = (s16[272,1024]{1,0:T(8,128)(2,1)S(1)}, s16[272,1024]{1,0:T(8,128)(2,1)S(1)}, u32[]{:S(2)}, u32[]{:S(2)}) collective-permute-start(s16[272,1024]{1,0:T(8,128)(2,1)S(1)} %collective-permute-done.15), channel_id=1, source_target_pairs={{0,32},{1,48},{2,35},{3,51},{4,4},{5,20},{6,7},{7,23},{8,40},{9,56... | collective-permute-start | bytes 1671176 | tf_op jit(solution)/shard_map/ppermute | solution.py:366
  138.1 2.1 %collective-permute-start.21 = (s16[272,1024]{1,0:T(8,128)(2,1)S(1)}, s16[272,1024]{1,0:T(8,128)(2,1)S(1)}, u32[]{:S(2)}, u32[]{:S(2)}) collective-permute-start(s16[272,1024]{1,0:T(8,128)(2,1)S(1)} %get-tuple-element.83), channel_id=1, source_target_pairs={{0,4},{1,6},{2,5},{3,7},{4,0},{5,2},{6,1},{7,3},{8,12},{9,14},{10,... | collective-permute-start | bytes 1671176 | tf_op jit(solution)/shard_map/ppermute | solution.py:366
  140.9 1.9 shard_map.70
  142.8 2.2 %collective-permute-done.19.refs_3_ = s16[272,1024]{1,0:T(8,128)(2,1)S(1)} collective-permute-done((s16[272,1024]{1,0:T(8,128)(2,1)S(1)}, s16[272,1024]{1,0:T(8,128)(2,1)S(1)}, u32[]{:S(2)}, u32[]{:S(2)}) %collective-permute-start.19) | collective-permute-done | bytes 557088 | tf_op jit(solution)/shard_map/ppermute | solution.py:366
  145.0 1.9 shard_map.71
  146.9 3.3 %collective-permute-done.12.refs_1_ = s16[256,2048]{1,0:T(8,128)(2,1)S(1)} collective-permute-done((s16[256,2048]{1,0:T(8,128)(2,1)S(1)}, s16[256,2048]{1,0:T(8,128)(2,1)S(1)}, u32[]{:S(2)}, u32[]{:S(2)}) %collective-permute-start.12) | collective-permute-done | bytes 1048608 | tf_op jit(solution)/shard_map/ppermute | solution.py:360
  150.2 1.6 copy-done
  151.8 1.5 shard_map.72
  154.7 8.1 %collective-permute-start.24 = (s16[272,1024]{1,0:T(8,128)(2,1)S(1)}, s16[272,1024]{1,0:T(8,128)(2,1)S(1)}, u32[]{:S(2)}, u32[]{:S(2)}) collective-permute-start(s16[272,1024]{1,0:T(8,128)(2,1)S(1)} %get-tuple-element.85), channel_id=1, source_target_pairs={{0,4},{1,6},{2,5},{3,7},{4,0},{5,2},{6,1},{7,3},{8,12},{9,14},{10,... | collective-permute-start | bytes 1671176 | tf_op jit(solution)/shard_map/ppermute | solution.py:366
  163.6 7.0 %collective-permute-start.27 = (s16[272,1024]{1,0:T(8,128)(2,1)S(1)}, s16[272,1024]{1,0:T(8,128)(2,1)S(1)}, u32[]{:S(2)}, u32[]{:S(2)}) collective-permute-start(s16[272,1024]{1,0:T(8,128)(2,1)S(1)} %collective-permute-done.21), channel_id=1, source_target_pairs={{0,32},{1,48},{2,35},{3,51},{4,4},{5,20},{6,7},{7,23},{8,40},{9,56... | collective-permute-start | bytes 1671176 | tf_op jit(solution)/shard_map/ppermute | solution.py:366
  171.3 2.5 %collective-permute-done.24 = s16[272,1024]{1,0:T(8,128)(2,1)S(1)} collective-permute-done((s16[272,1024]{1,0:T(8,128)(2,1)S(1)}, s16[272,1024]{1,0:T(8,128)(2,1)S(1)}, u32[]{:S(2)}, u32[]{:S(2)}) %collective-permute-start.24) | collective-permute-done | bytes 557088 | tf_op jit(solution)/shard_map/ppermute | solution.py:366
  173.8 8.0 %collective-permute-start.25 = (s16[272,1024]{1,0:T(8,128)(2,1)S(1)}, s16[272,1024]{1,0:T(8,128)(2,1)S(1)}, u32[]{:S(2)}, u32[]{:S(2)}) collective-permute-start(s16[272,1024]{1,0:T(8,128)(2,1)S(1)} %collective-permute-done.24), channel_id=1, source_target_pairs={{0,32},{1,48},{2,35},{3,51},{4,4},{5,20},{6,7},{7,23},{8,40},{9,56... | collective-permute-start | bytes 1671176 | tf_op jit(solution)/shard_map/ppermute | solution.py:366
  181.8 0.8 collective-permute-done.27.refs_3_
  182.6 1.9 shard_map.73
  184.5 6.2 %collective-permute-start.28 = (bf16[768,512]{1,0:T(8,128)(2,1)S(1)}, bf16[768,512]{1,0:T(8,128)(2,1)S(1)}, u32[]{:S(2)}, u32[]{:S(2)}) collective-permute-start(bf16[768,512]{1,0:T(8,128)(2,1)S(1)} %get-tuple-element.91), channel_id=1, source_target_pairs={{0,1},{1,0},{2,3},{3,2},{4,5},{5,4},{6,7},{7,6},{8,9},{9,8},{10,11... | collective-permute-start | bytes 2359304 | tf_op jit(solution)/shard_map/ppermute | solution.py:399
  190.7 4.5 %collective-permute-done.25.refs_3_ = s16[272,1024]{1,0:T(8,128)(2,1)S(1)} collective-permute-done((s16[272,1024]{1,0:T(8,128)(2,1)S(1)}, s16[272,1024]{1,0:T(8,128)(2,1)S(1)}, u32[]{:S(2)}, u32[]{:S(2)}) %collective-permute-start.25) | collective-permute-done | bytes 557088 | tf_op jit(solution)/shard_map/ppermute | solution.py:366
  195.3 1.9 shard_map.74
  197.2 5.2 %collective-permute-start.29 = (bf16[256,512]{1,0:T(8,128)(2,1)S(1)}, bf16[256,512]{1,0:T(8,128)(2,1)S(1)}, u32[]{:S(2)}, u32[]{:S(2)}) collective-permute-start(bf16[256,512]{1,0:T(8,128)(2,1)S(1)} %get-tuple-element.92), channel_id=1, source_target_pairs={{0,1},{1,0},{2,3},{3,2},{4,5},{5,4},{6,7},{7,6},{8,9},{9,8},{10,11... | collective-permute-start | bytes 786440 | tf_op jit(solution)/shard_map/ppermute | solution.py:401
  202.4 1.2 collective-permute-done.30.refs_5_
  203.6 1.5 shard_map.75
  (41 shorter events, 10.6 us)
Async XLA Ops:
  4.0 27.5 %copy-start.1 = (s32[8]{0:T(128)S(1)}, s32[8]{0:T(128)}, u32[]{:S(2)}) copy-start(s32[8]{0:T(128)} %refs_1_.19) | copy-start | bytes 100
  4.0 27.5 %collective-permute-start.1 = (bf16[272,4096]{1,0:T(8,128)(2,1)S(1)}, bf16[272,4096]{1,0:T(8,128)(2,1)S(1)}, u32[]{:S(2)}, u32[]{:S(2)}) collective-permute-start(bf16[272,4096]{1,0:T(8,128)(2,1)S(1)} %shard_map.60), channel_id=1, source_target_pairs={{0,16},{1,49},{2,18},{3,51},{4,20},{5,53},{6,22},{7,55},{8,24},{9,... | collective-permute-start | bytes 6684680 | tf_op jit(solution)/shard_map/ppermute | solution.py:351
  7.8 46.2 %collective-permute-start = (bf16[256,4096]{1,0:T(8,128)(2,1)S(1)}, bf16[256,4096]{1,0:T(8,128)(2,1)S(1)}, u32[]{:S(2)}, u32[]{:S(2)}) collective-permute-start(bf16[256,4096]{1,0:T(8,128)(2,1)S(1)} %shard_map.59), channel_id=1, source_target_pairs={{0,16},{1,49},{2,18},{3,51},{4,20},{5,53},{6,22},{7,55},{8,24},{9,... | collective-permute-start | bytes 6291464 | tf_op jit(solution)/shard_map/ppermute | solution.py:351
  35.6 28.0 %collective-permute-start.2 = (s16[272,2048]{1,0:T(8,128)(2,1)S(1)}, s16[272,2048]{1,0:T(8,128)(2,1)S(1)}, u32[]{:S(2)}, u32[]{:S(2)}) collective-permute-start(s16[272,2048]{1,0:T(8,128)(2,1)S(1)} %get-tuple-element.48.refs_10_.refs_3_), channel_id=1, source_target_pairs={{0,8},{1,9},{2,10},{3,11},{4,12},{5,13},{6,14},{7,15},{8,72},{9,73... | collective-permute-start | bytes 3342344 | tf_op jit(solution)/shard_map/ppermute | solution.py:360
  37.3 26.2 %collective-permute-start.3 = (s16[272,2048]{1,0:T(8,128)(2,1)S(1)}, s16[272,2048]{1,0:T(8,128)(2,1)S(1)}, u32[]{:S(2)}, u32[]{:S(2)}) collective-permute-start(s16[272,2048]{1,0:T(8,128)(2,1)S(1)} %get-tuple-element.49.refs_11_.refs_4_), channel_id=1, source_target_pairs={{0,0},{1,1},{2,2},{3,3},{4,4},{5,5},{6,6},{7,7},{8,64},{9,65},{10,... | collective-permute-start | bytes 3342344 | tf_op jit(solution)/shard_map/ppermute | solution.py:360
  40.2 36.3 %collective-permute-start.7 = (bf16[256,4096]{1,0:T(8,128)(2,1)S(1)}, bf16[256,4096]{1,0:T(8,128)(2,1)S(1)}, u32[]{:S(2)}, u32[]{:S(2)}) collective-permute-start(bf16[256,4096]{1,0:T(8,128)(2,1)S(1)} %shard_map.65), channel_id=1, source_target_pairs={{0,16},{1,49},{2,18},{3,51},{4,20},{5,53},{6,22},{7,55},{8,24},{9,... | collective-permute-start | bytes 6291464 | tf_op jit(solution)/shard_map/ppermute | solution.py:351
  67.3 35.3 %collective-permute-start.4 = (bf16[256,4096]{1,0:T(8,128)(2,1)S(1)}, bf16[256,4096]{1,0:T(8,128)(2,1)S(1)}, u32[]{:S(2)}, u32[]{:S(2)}) collective-permute-start(bf16[256,4096]{1,0:T(8,128)(2,1)S(1)} %shard_map.64), channel_id=1, source_target_pairs={{0,16},{1,49},{2,18},{3,51},{4,20},{5,53},{6,22},{7,55},{8,24},{9,... | collective-permute-start | bytes 6291464 | tf_op jit(solution)/shard_map/ppermute | solution.py:351
  68.0 28.1 %collective-permute-start.5 = (s16[256,2048]{1,0:T(8,128)(2,1)S(1)}, s16[256,2048]{1,0:T(8,128)(2,1)S(1)}, u32[]{:S(2)}, u32[]{:S(2)}) collective-permute-start(s16[256,2048]{1,0:T(8,128)(2,1)S(1)} %get-tuple-element.54.refs_5_.refs_3_.refs_10_), channel_id=1, source_target_pairs={{0,8},{1,9},{2,10},{3,11},{4,12},{5,13},{6,14},{7,15},{8,72},{9,73... | collective-permute-start | bytes 3145736 | tf_op jit(solution)/shard_map/ppermute | solution.py:360
  71.9 24.1 %collective-permute-start.6 = (s16[256,2048]{1,0:T(8,128)(2,1)S(1)}, s16[256,2048]{1,0:T(8,128)(2,1)S(1)}, u32[]{:S(2)}, u32[]{:S(2)}) collective-permute-start(s16[256,2048]{1,0:T(8,128)(2,1)S(1)} %get-tuple-element.55.refs_6_.refs_4_.refs_11_), channel_id=1, source_target_pairs={{0,0},{1,1},{2,2},{3,3},{4,4},{5,5},{6,6},{7,7},{8,64},{9,65},{10,... | collective-permute-start | bytes 3145736 | tf_op jit(solution)/shard_map/ppermute | solution.py:360
  72.7 24.9 %collective-permute-start.8 = (s16[288,1024]{1,0:T(8,128)(2,1)S(1)}, s16[288,1024]{1,0:T(8,128)(2,1)S(1)}, u32[]{:S(2)}, u32[]{:S(2)}) collective-permute-start(s16[288,1024]{1,0:T(8,128)(2,1)S(1)} %get-tuple-element.52.refs_5_.refs_12_), channel_id=1, source_target_pairs={{0,0},{1,2},{2,1},{3,3},{4,4},{5,6},{6,5},{7,7},{8,8},{9,10},{10,9... | collective-permute-start | bytes 1769480 | tf_op jit(solution)/shard_map/ppermute | solution.py:366
  76.4 21.1 %collective-permute-start.9 = (s16[288,1024]{1,0:T(8,128)(2,1)S(1)}, s16[288,1024]{1,0:T(8,128)(2,1)S(1)}, u32[]{:S(2)}, u32[]{:S(2)}) collective-permute-start(s16[288,1024]{1,0:T(8,128)(2,1)S(1)} %get-tuple-element.53.refs_6_.refs_13_), channel_id=1, source_target_pairs={{0,4},{1,6},{2,5},{3,7},{4,0},{5,2},{6,1},{7,3},{8,12},{9,14},{10,... | collective-permute-start | bytes 1769480 | tf_op jit(solution)/shard_map/ppermute | solution.py:366
  97.6 11.6 %collective-permute-start.14 = (s16[272,1024]{1,0:T(8,128)(2,1)S(1)}, s16[272,1024]{1,0:T(8,128)(2,1)S(1)}, u32[]{:S(2)}, u32[]{:S(2)}) collective-permute-start(s16[272,1024]{1,0:T(8,128)(2,1)S(1)} %get-tuple-element.68.refs_10_), channel_id=1, source_target_pairs={{0,0},{1,2},{2,1},{3,3},{4,4},{5,6},{6,5},{7,7},{8,8},{9,10},{10,9... | collective-permute-start | bytes 1671176 | tf_op jit(solution)/shard_map/ppermute | solution.py:366
  98.3 28.7 %collective-permute-start.10 = (s16[256,2048]{1,0:T(8,128)(2,1)S(1)}, s16[256,2048]{1,0:T(8,128)(2,1)S(1)}, u32[]{:S(2)}, u32[]{:S(2)}) collective-permute-start(s16[256,2048]{1,0:T(8,128)(2,1)S(1)} %get-tuple-element.62.refs_5_), channel_id=1, source_target_pairs={{0,8},{1,9},{2,10},{3,11},{4,12},{5,13},{6,14},{7,15},{8,72},{9,73... | collective-permute-start | bytes 3145736 | tf_op jit(solution)/shard_map/ppermute | solution.py:360
  101.8 25.2 %collective-permute-start.11 = (s16[256,2048]{1,0:T(8,128)(2,1)S(1)}, s16[256,2048]{1,0:T(8,128)(2,1)S(1)}, u32[]{:S(2)}, u32[]{:S(2)}) collective-permute-start(s16[256,2048]{1,0:T(8,128)(2,1)S(1)} %get-tuple-element.63.refs_6_), channel_id=1, source_target_pairs={{0,0},{1,1},{2,2},{3,3},{4,4},{5,5},{6,6},{7,7},{8,64},{9,65},{10,... | collective-permute-start | bytes 3145736 | tf_op jit(solution)/shard_map/ppermute | solution.py:360
  102.6 19.7 %collective-permute-start.16 = (s16[288,1024]{1,0:T(8,128)(2,1)S(1)}, s16[288,1024]{1,0:T(8,128)(2,1)S(1)}, u32[]{:S(2)}, u32[]{:S(2)}) collective-permute-start(s16[288,1024]{1,0:T(8,128)(2,1)S(1)} %collective-permute-done.8.refs_12_), channel_id=1, source_target_pairs={{0,0},{1,16},{2,3},{3,19},{4,36},{5,52},{6,39},{7,55},{8,8},{9,24}... | collective-permute-start | bytes 1769480 | tf_op jit(solution)/shard_map/ppermute | solution.py:366
  103.3 19.0 %collective-permute-start.17 = (s16[288,1024]{1,0:T(8,128)(2,1)S(1)}, s16[288,1024]{1,0:T(8,128)(2,1)S(1)}, u32[]{:S(2)}, u32[]{:S(2)}) collective-permute-start(s16[288,1024]{1,0:T(8,128)(2,1)S(1)} %collective-permute-done.9.refs_13_), channel_id=1, source_target_pairs={{0,32},{1,48},{2,35},{3,51},{4,4},{5,20},{6,7},{7,23},{8,40},{9,56... | collective-permute-start | bytes 1769480 | tf_op jit(solution)/shard_map/ppermute | solution.py:366
  109.2 13.0 %collective-permute-start.15 = (s16[272,1024]{1,0:T(8,128)(2,1)S(1)}, s16[272,1024]{1,0:T(8,128)(2,1)S(1)}, u32[]{:S(2)}, u32[]{:S(2)}) collective-permute-start(s16[272,1024]{1,0:T(8,128)(2,1)S(1)} %get-tuple-element.69.refs_11_), channel_id=1, source_target_pairs={{0,4},{1,6},{2,5},{3,7},{4,0},{5,2},{6,1},{7,3},{8,12},{9,14},{10,... | collective-permute-start | bytes 1671176 | tf_op jit(solution)/shard_map/ppermute | solution.py:366
  122.3 15.8 %collective-permute-start.18 = (s16[272,1024]{1,0:T(8,128)(2,1)S(1)}, s16[272,1024]{1,0:T(8,128)(2,1)S(1)}, u32[]{:S(2)}, u32[]{:S(2)}) collective-permute-start(s16[272,1024]{1,0:T(8,128)(2,1)S(1)} %collective-permute-done.14), channel_id=1, source_target_pairs={{0,0},{1,16},{2,3},{3,19},{4,36},{5,52},{6,39},{7,55},{8,8},{9,24}... | collective-permute-start | bytes 1671176 | tf_op jit(solution)/shard_map/ppermute | solution.py:366
  128.6 21.6 %collective-permute-start.12 = (s16[256,2048]{1,0:T(8,128)(2,1)S(1)}, s16[256,2048]{1,0:T(8,128)(2,1)S(1)}, u32[]{:S(2)}, u32[]{:S(2)}) collective-permute-start(s16[256,2048]{1,0:T(8,128)(2,1)S(1)} %get-tuple-element.66.refs_5_), channel_id=1, source_target_pairs={{0,8},{1,9},{2,10},{3,11},{4,12},{5,13},{6,14},{7,15},{8,72},{9,73... | collective-permute-start | bytes 3145736 | tf_op jit(solution)/shard_map/ppermute | solution.py:360
  130.5 19.7 %collective-permute-start.13 = (s16[256,2048]{1,0:T(8,128)(2,1)S(1)}, s16[256,2048]{1,0:T(8,128)(2,1)S(1)}, u32[]{:S(2)}, u32[]{:S(2)}) collective-permute-start(s16[256,2048]{1,0:T(8,128)(2,1)S(1)} %get-tuple-element.67.refs_6_), channel_id=1, source_target_pairs={{0,0},{1,1},{2,2},{3,3},{4,4},{5,5},{6,6},{7,7},{8,64},{9,65},{10,... | collective-permute-start | bytes 3145736 | tf_op jit(solution)/shard_map/ppermute | solution.py:360
  131.2 13.8 %collective-permute-start.19 = (s16[272,1024]{1,0:T(8,128)(2,1)S(1)}, s16[272,1024]{1,0:T(8,128)(2,1)S(1)}, u32[]{:S(2)}, u32[]{:S(2)}) collective-permute-start(s16[272,1024]{1,0:T(8,128)(2,1)S(1)} %collective-permute-done.15), channel_id=1, source_target_pairs={{0,32},{1,48},{2,35},{3,51},{4,4},{5,20},{6,7},{7,23},{8,40},{9,56... | collective-permute-start | bytes 1671176 | tf_op jit(solution)/shard_map/ppermute | solution.py:366
  137.4 16.0 %collective-permute-start.20 = (s16[272,1024]{1,0:T(8,128)(2,1)S(1)}, s16[272,1024]{1,0:T(8,128)(2,1)S(1)}, u32[]{:S(2)}, u32[]{:S(2)}) collective-permute-start(s16[272,1024]{1,0:T(8,128)(2,1)S(1)} %get-tuple-element.82), channel_id=1, source_target_pairs={{0,0},{1,2},{2,1},{3,3},{4,4},{5,6},{6,5},{7,7},{8,8},{9,10},{10,9... | collective-permute-start | bytes 1671176 | tf_op jit(solution)/shard_map/ppermute | solution.py:366
  138.1 15.9 %collective-permute-start.21 = (s16[272,1024]{1,0:T(8,128)(2,1)S(1)}, s16[272,1024]{1,0:T(8,128)(2,1)S(1)}, u32[]{:S(2)}, u32[]{:S(2)}) collective-permute-start(s16[272,1024]{1,0:T(8,128)(2,1)S(1)} %get-tuple-element.83), channel_id=1, source_target_pairs={{0,4},{1,6},{2,5},{3,7},{4,0},{5,2},{6,1},{7,3},{8,12},{9,14},{10,... | collective-permute-start | bytes 1671176 | tf_op jit(solution)/shard_map/ppermute | solution.py:366
  150.2 1.6 copy-start
  154.0 16.6 %collective-permute-start.22 = (s16[272,1024]{1,0:T(8,128)(2,1)S(1)}, s16[272,1024]{1,0:T(8,128)(2,1)S(1)}, u32[]{:S(2)}, u32[]{:S(2)}) collective-permute-start(s16[272,1024]{1,0:T(8,128)(2,1)S(1)} %get-tuple-element.84), channel_id=1, source_target_pairs={{0,0},{1,2},{2,1},{3,3},{4,4},{5,6},{6,5},{7,7},{8,8},{9,10},{10,9... | collective-permute-start | bytes 1671176 | tf_op jit(solution)/shard_map/ppermute | solution.py:366
  154.7 19.1 %collective-permute-start.24 = (s16[272,1024]{1,0:T(8,128)(2,1)S(1)}, s16[272,1024]{1,0:T(8,128)(2,1)S(1)}, u32[]{:S(2)}, u32[]{:S(2)}) collective-permute-start(s16[272,1024]{1,0:T(8,128)(2,1)S(1)} %get-tuple-element.85), channel_id=1, source_target_pairs={{0,4},{1,6},{2,5},{3,7},{4,0},{5,2},{6,1},{7,3},{8,12},{9,14},{10,... | collective-permute-start | bytes 1671176 | tf_op jit(solution)/shard_map/ppermute | solution.py:366
  162.9 18.9 %collective-permute-start.26 = (s16[272,1024]{1,0:T(8,128)(2,1)S(1)}, s16[272,1024]{1,0:T(8,128)(2,1)S(1)}, u32[]{:S(2)}, u32[]{:S(2)}) collective-permute-start(s16[272,1024]{1,0:T(8,128)(2,1)S(1)} %collective-permute-done.20), channel_id=1, source_target_pairs={{0,0},{1,16},{2,3},{3,19},{4,36},{5,52},{6,39},{7,55},{8,8},{9,24}... | collective-permute-start | bytes 1671176 | tf_op jit(solution)/shard_map/ppermute | solution.py:366
  163.6 19.0 %collective-permute-start.27 = (s16[272,1024]{1,0:T(8,128)(2,1)S(1)}, s16[272,1024]{1,0:T(8,128)(2,1)S(1)}, u32[]{:S(2)}, u32[]{:S(2)}) collective-permute-start(s16[272,1024]{1,0:T(8,128)(2,1)S(1)} %collective-permute-done.21), channel_id=1, source_target_pairs={{0,32},{1,48},{2,35},{3,51},{4,4},{5,20},{6,7},{7,23},{8,40},{9,56... | collective-permute-start | bytes 1671176 | tf_op jit(solution)/shard_map/ppermute | solution.py:366
  170.6 20.1 %collective-permute-start.23 = (s16[272,1024]{1,0:T(8,128)(2,1)S(1)}, s16[272,1024]{1,0:T(8,128)(2,1)S(1)}, u32[]{:S(2)}, u32[]{:S(2)}) collective-permute-start(s16[272,1024]{1,0:T(8,128)(2,1)S(1)} %collective-permute-done.22), channel_id=1, source_target_pairs={{0,0},{1,16},{2,3},{3,19},{4,36},{5,52},{6,39},{7,55},{8,8},{9,24}... | collective-permute-start | bytes 1671176 | tf_op jit(solution)/shard_map/ppermute | solution.py:366
  173.8 21.5 %collective-permute-start.25 = (s16[272,1024]{1,0:T(8,128)(2,1)S(1)}, s16[272,1024]{1,0:T(8,128)(2,1)S(1)}, u32[]{:S(2)}, u32[]{:S(2)}) collective-permute-start(s16[272,1024]{1,0:T(8,128)(2,1)S(1)} %collective-permute-done.24), channel_id=1, source_target_pairs={{0,32},{1,48},{2,35},{3,51},{4,4},{5,20},{6,7},{7,23},{8,40},{9,56... | collective-permute-start | bytes 1671176 | tf_op jit(solution)/shard_map/ppermute | solution.py:366
  184.5 19.0 %collective-permute-start.28 = (bf16[768,512]{1,0:T(8,128)(2,1)S(1)}, bf16[768,512]{1,0:T(8,128)(2,1)S(1)}, u32[]{:S(2)}, u32[]{:S(2)}) collective-permute-start(bf16[768,512]{1,0:T(8,128)(2,1)S(1)} %get-tuple-element.91), channel_id=1, source_target_pairs={{0,1},{1,0},{2,3},{3,2},{4,5},{5,4},{6,7},{7,6},{8,9},{9,8},{10,11... | collective-permute-start | bytes 2359304 | tf_op jit(solution)/shard_map/ppermute | solution.py:399
  197.2 6.3 %collective-permute-start.29 = (bf16[256,512]{1,0:T(8,128)(2,1)S(1)}, bf16[256,512]{1,0:T(8,128)(2,1)S(1)}, u32[]{:S(2)}, u32[]{:S(2)}) collective-permute-start(bf16[256,512]{1,0:T(8,128)(2,1)S(1)} %get-tuple-element.92), channel_id=1, source_target_pairs={{0,1},{1,0},{2,3},{3,2},{4,5},{5,4},{6,7},{7,6},{8,9},{9,8},{10,11... | collective-permute-start | bytes 786440 | tf_op jit(solution)/shard_map/ppermute | solution.py:401
  202.4 1.2 collective-permute-start.30

commit v3 on v2

--- a/solution.py
+++ b/solution.py
@@ -10,6 +10,7 @@
 AXES = ("ckpt", "row")
 OWN, PARTNER, KEEP, YHI, SLOT, CORE = range(6)
 TILE = 512
+WIDTH = 1024
 ROWS = 1024
 CHUNK = 256
 CHUNKS = ROWS // CHUNK
@@ -145,7 +146,7 @@
             for band in range(BANDS):
                 row = chunk * BANDS + band
                 rows = pl.ds(band * BLOCK, BLOCK)
-                for col in range(TILE // BLOCK):
+                for col in range(WIDTH // BLOCK):
                     cols = slice(col * BLOCK, (col + 1) * BLOCK)
                     total = (
                         kept[0, rows, cols].astype(jnp.float32) * own[row : row + 1, cols]
@@ -155,26 +156,23 @@
             if extra:
                 out[pl.ds(CHUNK, UNITS), :] = unit.astype(jnp.int16)
 
-    def kept_col(y_lo, t):
-        return lambda p: 2 * (y_lo(p) * 4 + p[KEEP] + 2 * (t // 2)) + t % 2
-
     far, near = (lambda p: 1 - p[YHI]), (lambda p: p[YHI])
 
     def kept_at(y_lo, row):
-        return lambda t, p, w: (*row, 2 * (y_lo(p) * 4 + p[KEEP] + 2 * (t // 2)) + t % 2)
+        return lambda t, p, w: (*row, y_lo(p) * 4 + p[KEEP] + 2 * t)
 
     def came_at(y_lo, row):
-        return lambda t, p, w: (row, y_lo(p) * 4 + t)
-
-    sent = (CHUNK + extra, TILE)
+        return lambda t, p, w: (row, y_lo(p) * 2 + t)
+
+    sent = (CHUNK + extra, WIDTH)
     return call(
         kernel,
-        (4,),
+        (2,),
         [place, weights],
-        [(codes, pl.BlockSpec((1, CHUNK, TILE), kept_at(y, (0, chunk)))) for y in (far, near)]
-        + [(received, pl.BlockSpec((CHUNK, TILE), came_at(y, 0))) for y in (far, near)]
-        + [(wide_exps, pl.BlockSpec((UNITS, TILE), kept_at(y, (0,)))) for y in (far, near)]
-        + [(first_received, pl.BlockSpec((UNITS, TILE), came_at(y, CHUNK // UNITS))) for y in (far, near)],
+        [(codes, pl.BlockSpec((1, CHUNK, WIDTH), kept_at(y, (0, chunk)))) for y in (far, near)]
+        + [(received, pl.BlockSpec((CHUNK, WIDTH), came_at(y, 0))) for y in (far, near)]
+        + [(wide_exps, pl.BlockSpec((UNITS, WIDTH), kept_at(y, (0,)))) for y in (far, near)]
+        + [(first_received, pl.BlockSpec((UNITS, WIDTH), came_at(y, CHUNK // UNITS))) for y in (far, near)],
         [((CHUNK + extra, 4 * TILE), jnp.int16, pl.BlockSpec(sent, lambda t, *_: (0, t)))] * 2,
         after,
     )
@@ -384,7 +382,7 @@
     moved[2] = move_y(pairs[2], fours[1])
     parts[1] = move(fours[1], Z_PERMS, parts[0])
     pairs[3] = pairs_of(3, (*fours[1], *parts[0]))
-    parts[0] = move(parts[0], X_PERMS, received[3])
+    parts[0] = move(parts[0], X_PERMS, pairs[3])
     fours[2] = fours_of(2, pairs[3])
     moved[3] = move_y(pairs[3], fours[2])
     parts[2] = move(fours[2], Z_PERMS, parts[1])

time: 208 us -> 207 us (level)
  Pallas kernels: 40.2 us -> 37.2 us
    pallas_call x17, Pallas kernels: 40.2 us -> 37.2 us  [call(): pl.pallas_call(whole, grid_spec=pltpu.PrefetchScalarGridSpec(num_scalar_p...]
    ppermute x16, waiting for transfers between devices: 21.9 us -> 24.1 us  [move(): lax.ppermute(part, AXES, perm)]
  transfers between devices with their start and end apart: 31 -> 31, of which waited for: 13 -> 12; matrix products, arithmetic and copies ran while one was open for 0% -> 0% of each run, Pallas kernels for 18% -> 16%
where the time goes in v3:
time: 207 us; the launch traced here: 203 us
  waiting for transfers between devices  81.7 us (39%)
  starting transfers between devices  79.4 us (38%)
  Pallas kernels  37.2 us (18%)
  local copies, waits for them, and re-layouts  2.59 us (1%)
    ppermute x16, starting transfers between devices, move(): lax.ppermute(part, AXES, perm)  50.5 us
    ppermute x4, waiting for transfers between devices, swap_pairs(): lax.ppermute(pack(chunk, place, quant_codes, wide_exps, after), AXES, PAI...  40 us
    pallas_call x17, Pallas kernels, call(): pl.pallas_call(whole, grid_spec=pltpu.PrefetchScalarGridSpec(num_scalar_p...  37.2 us
    ppermute x16, waiting for transfers between devices, move(): lax.ppermute(part, AXES, perm)  24.1 us
    ppermute x4, waiting for transfers between devices, move_y(): lax.ppermute(far, AXES, ACROSS_PERM)  16.4 us
    ppermute x4, starting transfers between devices, move_y(): lax.ppermute(far, AXES, ACROSS_PERM)  11.1 us
    ppermute x1, starting transfers between devices, body(): came = lax.ppermute(done[1], AXES, CORE_PERM)  6 us
    ppermute x1, starting transfers between devices, body(): last_came = lax.ppermute(other, AXES, CORE_PERM)  4.48 us
  transfers between devices with their start and end apart: 31, of which 12 were waited for; matrix products, arithmetic and copies ran while one was open for 0% of the time, Pallas kernels for 16%

profile of v3, /device:TPU:0, one launch (start us, length us, event | category | flops | bytes accessed | tf_op | source)
XLA Modules:
  0.0 203.4 jit_solution(642963367785684021)
XLA Ops:
  1.8 2.2 %shard_map.60 = bf16[272,4096]{1,0:T(8,128)(2,1)S(1)} custom-call(s32[6]{0:T(128)S(1)} %stack.27.refs_0_, bf16[1,1024,8192]{2,1,0:T(8,128)(2,1)} %refs_3_.7, bf16[16,8192]{1,0:T(8,128)(2,1)S(1)} %pad.5.refs_2_.refs_6_.refs_7_), custom_call_target="tpu_custom_call" | custom-call | bytes 17039360 | tf_op jit(solution)/shard_map/pallas_call | solution.py:68
  4.0 1.7 collective-permute-start.1
  5.6 2.1 %shard_map.59 = bf16[256,4096]{1,0:T(8,128)(2,1)S(1)} custom-call(s32[6]{0:T(128)S(1)} %stack.27.refs_0_, bf16[1,1024,8192]{2,1,0:T(8,128)(2,1)} %refs_3_.7, bf16[16,8192]{1,0:T(8,128)(2,1)S(1)} %pad.5.refs_2_.refs_6_.refs_7_), custom_call_target="tpu_custom_call" | custom-call | bytes 17039360 | tf_op jit(solution)/shard_map/pallas_call | solution.py:68
  8.3 23.2 %collective-permute-done.1.refs_4_.refs_5_.refs_8_.refs_9_ = bf16[272,4096]{1,0:T(8,128)(2,1)S(1)} collective-permute-done((bf16[272,4096]{1,0:T(8,128)(2,1)S(1)}, bf16[272,4096]{1,0:T(8,128)(2,1)S(1)}, u32[]{:S(2)}, u32[]{:S(2)}) %collective-permute-start.1) | collective-permute-done | bytes 2228256 | tf_op jit(solution)/shard_map/ppermute | solution.py:349
  31.5 3.3 %shard_map.61 = (s16[272,2048]{1,0:T(8,128)(2,1)S(1)}, s16[272,2048]{1,0:T(8,128)(2,1)S(1)}) custom-call(s32[6]{0:T(128)S(1)} %stack.27.refs_0_, s32[8]{0:T(128)S(1)} %copy-done.1, bf16[1,1024,8192]{2,1,0:T(8,128)(2,1)} %refs_3_.7, bf16[1,1024,8192]{2,1,0:T(8,128)(2,1)} %refs_3_.7, ...), custom_call_target="tpu_custom_call" | custom-call | bytes 42991616 | tf_op jit(solution)/shard_map/pallas_call | solution.py:68
  34.8 1.7 collective-permute-start.2
  36.6 0.7 collective-permute-start.3
  37.3 2.1 %shard_map.65 = bf16[256,4096]{1,0:T(8,128)(2,1)S(1)} custom-call(s32[6]{0:T(128)S(1)} %stack.27.refs_0_, bf16[1,1024,8192]{2,1,0:T(8,128)(2,1)} %refs_3_.7, bf16[16,8192]{1,0:T(8,128)(2,1)S(1)} %pad.5.refs_2_.refs_6_.refs_7_, s16[272,2048]{1,0:T(8,128)(2,1)S(1)} %get-tuple-element.48.refs_10_.refs_3_, s16[272,2048]{1,0:T(8,128)(2,1)S(1)} %get-tuple-element.49.refs_11_.refs_4_), custom_call_target="tpu_custom_call" | custom-call | bytes 17039360 | tf_op jit(solution)/shard_map/pallas_call | solution.py:68
  39.4 1.6 collective-permute-start.7
  41.0 13.0 %collective-permute-done.refs_4_.refs_5_ = bf16[256,4096]{1,0:T(8,128)(2,1)S(1)} collective-permute-done((bf16[256,4096]{1,0:T(8,128)(2,1)S(1)}, bf16[256,4096]{1,0:T(8,128)(2,1)S(1)}, u32[]{:S(2)}, u32[]{:S(2)}) %collective-permute-start) | collective-permute-done | bytes 2097184 | tf_op jit(solution)/shard_map/ppermute | solution.py:349
  54.0 3.3 %shard_map.62 = (s16[256,2048]{1,0:T(8,128)(2,1)S(1)}, s16[256,2048]{1,0:T(8,128)(2,1)S(1)}) custom-call(s32[6]{0:T(128)S(1)} %stack.27.refs_0_, s32[8]{0:T(128)S(1)} %copy-done.1, bf16[1,1024,8192]{2,1,0:T(8,128)(2,1)} %refs_3_.7, bf16[1,1024,8192]{2,1,0:T(8,128)(2,1)} %refs_3_.7, bf16[256,4096]{1,0:T(8,128)(2,1)S(1)} %collective-permute-done.refs_4_.refs_5_, ...), custom_call_target="tpu_custom_call" | custom-call | bytes 42729472 | tf_op jit(solution)/shard_map/pallas_call | solution.py:68
  57.3 5.5 %collective-permute-done.2.refs_1_.refs_3_ = s16[272,2048]{1,0:T(8,128)(2,1)S(1)} collective-permute-done((s16[272,2048]{1,0:T(8,128)(2,1)S(1)}, s16[272,2048]{1,0:T(8,128)(2,1)S(1)}, u32[]{:S(2)}, u32[]{:S(2)}) %collective-permute-start.2) | collective-permute-done | bytes 1114144 | tf_op jit(solution)/shard_map/ppermute | solution.py:358
  62.8 1.6 shard_map.63
  64.4 2.1 %shard_map.64 = bf16[256,4096]{1,0:T(8,128)(2,1)S(1)} custom-call(s32[6]{0:T(128)S(1)} %stack.27.refs_0_, bf16[1,1024,8192]{2,1,0:T(8,128)(2,1)} %refs_3_.7, bf16[16,8192]{1,0:T(8,128)(2,1)S(1)} %pad.5.refs_2_.refs_6_.refs_7_, s16[256,2048]{1,0:T(8,128)(2,1)S(1)} %get-tuple-element.54.refs_5_.refs_3_.refs_10_, ...), custom_call_target="tpu_custom_call" | custom-call | bytes 17039360 | tf_op jit(solution)/shard_map/pallas_call | solution.py:68
  67.2 4.0 %collective-permute-start.5 = (s16[256,2048]{1,0:T(8,128)(2,1)S(1)}, s16[256,2048]{1,0:T(8,128)(2,1)S(1)}, u32[]{:S(2)}, u32[]{:S(2)}) collective-permute-start(s16[256,2048]{1,0:T(8,128)(2,1)S(1)} %get-tuple-element.54.refs_5_.refs_3_.refs_10_), channel_id=1, source_target_pairs={{0,8},{1,9},{2,10},{3,11},{4,12},{5,13},{6,14},{7,15},{8,72},{9,73... | collective-permute-start | bytes 3145736 | tf_op jit(solution)/shard_map/ppermute | solution.py:358
  71.2 0.7 collective-permute-start.6
  72.6 3.8 %collective-permute-done.7.refs_4_.refs_5_ = bf16[256,4096]{1,0:T(8,128)(2,1)S(1)} collective-permute-done((bf16[256,4096]{1,0:T(8,128)(2,1)S(1)}, bf16[256,4096]{1,0:T(8,128)(2,1)S(1)}, u32[]{:S(2)}, u32[]{:S(2)}) %collective-permute-start.7) | collective-permute-done | bytes 2097184 | tf_op jit(solution)/shard_map/ppermute | solution.py:349
  76.4 5.9 %collective-permute-start.9 = (s16[288,1024]{1,0:T(8,128)(2,1)S(1)}, s16[288,1024]{1,0:T(8,128)(2,1)S(1)}, u32[]{:S(2)}, u32[]{:S(2)}) collective-permute-start(s16[288,1024]{1,0:T(8,128)(2,1)S(1)} %get-tuple-element.53.refs_6_.refs_13_), channel_id=1, source_target_pairs={{0,4},{1,6},{2,5},{3,7},{4,0},{5,2},{6,1},{7,3},{8,12},{9,14},{10,... | collective-permute-start | bytes 1769480 | tf_op jit(solution)/shard_map/ppermute | solution.py:364
  82.3 3.3 %shard_map.66 = (s16[256,2048]{1,0:T(8,128)(2,1)S(1)}, s16[256,2048]{1,0:T(8,128)(2,1)S(1)}) custom-call(s32[6]{0:T(128)S(1)} %stack.27.refs_0_, s32[8]{0:T(128)S(1)} %copy-done.1, bf16[1,1024,8192]{2,1,0:T(8,128)(2,1)} %refs_3_.7, bf16[1,1024,8192]{2,1,0:T(8,128)(2,1)} %refs_3_.7, bf16[256,4096]{1,0:T(8,128)(2,1)S(1)} %collective-permute-done.7.refs_4_.refs_5_, ...), custom_call_target="tpu_custom_call" | custom-call | bytes 42729472 | tf_op jit(solution)/shard_map/pallas_call | solution.py:68
  85.6 9.7 %collective-permute-done.5.refs_1_ = s16[256,2048]{1,0:T(8,128)(2,1)S(1)} collective-permute-done((s16[256,2048]{1,0:T(8,128)(2,1)S(1)}, s16[256,2048]{1,0:T(8,128)(2,1)S(1)}, u32[]{:S(2)}, u32[]{:S(2)}) %collective-permute-start.5) | collective-permute-done | bytes 1048608 | tf_op jit(solution)/shard_map/ppermute | solution.py:358
  95.3 1.5 shard_map.67
  97.6 3.5 %collective-permute-start.10 = (s16[256,2048]{1,0:T(8,128)(2,1)S(1)}, s16[256,2048]{1,0:T(8,128)(2,1)S(1)}, u32[]{:S(2)}, u32[]{:S(2)}) collective-permute-start(s16[256,2048]{1,0:T(8,128)(2,1)S(1)} %get-tuple-element.62.refs_5_), channel_id=1, source_target_pairs={{0,8},{1,9},{2,10},{3,11},{4,12},{5,13},{6,14},{7,15},{8,72},{9,73... | collective-permute-start | bytes 3145736 | tf_op jit(solution)/shard_map/ppermute | solution.py:358
  101.1 0.7 collective-permute-start.11
  101.8 3.3 %shard_map.68 = (s16[256,2048]{1,0:T(8,128)(2,1)S(1)}, s16[256,2048]{1,0:T(8,128)(2,1)S(1)}) custom-call(s32[6]{0:T(128)S(1)} %stack.27.refs_0_, s32[8]{0:T(128)S(1)} %copy-done.1, bf16[1,1024,8192]{2,1,0:T(8,128)(2,1)} %refs_3_.7, bf16[1,1024,8192]{2,1,0:T(8,128)(2,1)} %refs_3_.7, bf16[256,4096]{1,0:T(8,128)(2,1)S(1)} %collective-permute-done.4.refs_4_.refs_5_, ...), custom_call_target="tpu_custom_call" | custom-call | bytes 42729472 | tf_op jit(solution)/shard_map/pallas_call | solution.py:68
  105.8 5.9 %collective-permute-start.17 = (s16[288,1024]{1,0:T(8,128)(2,1)S(1)}, s16[288,1024]{1,0:T(8,128)(2,1)S(1)}, u32[]{:S(2)}, u32[]{:S(2)}) collective-permute-start(s16[288,1024]{1,0:T(8,128)(2,1)S(1)} %collective-permute-done.9.refs_13_), channel_id=1, source_target_pairs={{0,32},{1,48},{2,35},{3,51},{4,4},{5,20},{6,7},{7,23},{8,40},{9,56... | collective-permute-start | bytes 1769480 | tf_op jit(solution)/shard_map/ppermute | solution.py:364
  111.8 1.9 collective-permute-start.15
  113.7 11.1 %collective-permute-done.15 = s16[272,1024]{1,0:T(8,128)(2,1)S(1)} collective-permute-done((s16[272,1024]{1,0:T(8,128)(2,1)S(1)}, s16[272,1024]{1,0:T(8,128)(2,1)S(1)}, u32[]{:S(2)}, u32[]{:S(2)}) %collective-permute-start.15) | collective-permute-done | bytes 557088 | tf_op jit(solution)/shard_map/ppermute | solution.py:364
  125.6 1.5 shard_map.69
  127.1 1.8 collective-permute-start.12
  129.7 6.9 %collective-permute-start.19 = (s16[272,1024]{1,0:T(8,128)(2,1)S(1)}, s16[272,1024]{1,0:T(8,128)(2,1)S(1)}, u32[]{:S(2)}, u32[]{:S(2)}) collective-permute-start(s16[272,1024]{1,0:T(8,128)(2,1)S(1)} %collective-permute-done.15), channel_id=1, source_target_pairs={{0,32},{1,48},{2,35},{3,51},{4,4},{5,20},{6,7},{7,23},{8,40},{9,56... | collective-permute-start | bytes 1671176 | tf_op jit(solution)/shard_map/ppermute | solution.py:364
  137.4 6.2 %collective-permute-start.21 = (s16[272,1024]{1,0:T(8,128)(2,1)S(1)}, s16[272,1024]{1,0:T(8,128)(2,1)S(1)}, u32[]{:S(2)}, u32[]{:S(2)}) collective-permute-start(s16[272,1024]{1,0:T(8,128)(2,1)S(1)} %get-tuple-element.83), channel_id=1, source_target_pairs={{0,4},{1,6},{2,5},{3,7},{4,0},{5,2},{6,1},{7,3},{8,12},{9,14},{10,... | collective-permute-start | bytes 1671176 | tf_op jit(solution)/shard_map/ppermute | solution.py:364
  144.2 1.9 shard_map.70
  146.1 1.9 shard_map.71
  148.1 1.2 collective-permute-done.12.refs_1_
  149.2 1.6 copy-done
  150.8 1.5 shard_map.72
  152.4 4.4 %collective-permute-done.21 = s16[272,1024]{1,0:T(8,128)(2,1)S(1)} collective-permute-done((s16[272,1024]{1,0:T(8,128)(2,1)S(1)}, s16[272,1024]{1,0:T(8,128)(2,1)S(1)}, u32[]{:S(2)}, u32[]{:S(2)}) %collective-permute-start.21) | collective-permute-done | bytes 557088 | tf_op jit(solution)/shard_map/ppermute | solution.py:364
  157.5 3.9 %collective-permute-start.24 = (s16[272,1024]{1,0:T(8,128)(2,1)S(1)}, s16[272,1024]{1,0:T(8,128)(2,1)S(1)}, u32[]{:S(2)}, u32[]{:S(2)}) collective-permute-start(s16[272,1024]{1,0:T(8,128)(2,1)S(1)} %get-tuple-element.85), channel_id=1, source_target_pairs={{0,4},{1,6},{2,5},{3,7},{4,0},{5,2},{6,1},{7,3},{8,12},{9,14},{10,... | collective-permute-start | bytes 1671176 | tf_op jit(solution)/shard_map/ppermute | solution.py:364
  162.1 6.8 %collective-permute-start.27 = (s16[272,1024]{1,0:T(8,128)(2,1)S(1)}, s16[272,1024]{1,0:T(8,128)(2,1)S(1)}, u32[]{:S(2)}, u32[]{:S(2)}) collective-permute-start(s16[272,1024]{1,0:T(8,128)(2,1)S(1)} %collective-permute-done.21), channel_id=1, source_target_pairs={{0,32},{1,48},{2,35},{3,51},{4,4},{5,20},{6,7},{7,23},{8,40},{9,56... | collective-permute-start | bytes 1671176 | tf_op jit(solution)/shard_map/ppermute | solution.py:364
  169.6 3.0 %collective-permute-done.24 = s16[272,1024]{1,0:T(8,128)(2,1)S(1)} collective-permute-done((s16[272,1024]{1,0:T(8,128)(2,1)S(1)}, s16[272,1024]{1,0:T(8,128)(2,1)S(1)}, u32[]{:S(2)}, u32[]{:S(2)}) %collective-permute-start.24) | collective-permute-done | bytes 557088 | tf_op jit(solution)/shard_map/ppermute | solution.py:364
  172.6 7.5 %collective-permute-start.25 = (s16[272,1024]{1,0:T(8,128)(2,1)S(1)}, s16[272,1024]{1,0:T(8,128)(2,1)S(1)}, u32[]{:S(2)}, u32[]{:S(2)}) collective-permute-start(s16[272,1024]{1,0:T(8,128)(2,1)S(1)} %collective-permute-done.24), channel_id=1, source_target_pairs={{0,32},{1,48},{2,35},{3,51},{4,4},{5,20},{6,7},{7,23},{8,40},{9,56... | collective-permute-start | bytes 1671176 | tf_op jit(solution)/shard_map/ppermute | solution.py:364
  180.4 1.9 shard_map.73
  182.4 6.0 %collective-permute-start.28 = (bf16[768,512]{1,0:T(8,128)(2,1)S(1)}, bf16[768,512]{1,0:T(8,128)(2,1)S(1)}, u32[]{:S(2)}, u32[]{:S(2)}) collective-permute-start(bf16[768,512]{1,0:T(8,128)(2,1)S(1)} %get-tuple-element.91), channel_id=1, source_target_pairs={{0,1},{1,0},{2,3},{3,2},{4,5},{5,4},{6,7},{7,6},{8,9},{9,8},{10,11... | collective-permute-start | bytes 2359304 | tf_op jit(solution)/shard_map/ppermute | solution.py:397
  188.4 5.2 %collective-permute-done.25.refs_3_ = s16[272,1024]{1,0:T(8,128)(2,1)S(1)} collective-permute-done((s16[272,1024]{1,0:T(8,128)(2,1)S(1)}, s16[272,1024]{1,0:T(8,128)(2,1)S(1)}, u32[]{:S(2)}, u32[]{:S(2)}) %collective-permute-start.25) | collective-permute-done | bytes 557088 | tf_op jit(solution)/shard_map/ppermute | solution.py:364
  193.6 1.9 shard_map.74
  195.5 4.5 %collective-permute-start.29 = (bf16[256,512]{1,0:T(8,128)(2,1)S(1)}, bf16[256,512]{1,0:T(8,128)(2,1)S(1)}, u32[]{:S(2)}, u32[]{:S(2)}) collective-permute-start(bf16[256,512]{1,0:T(8,128)(2,1)S(1)} %get-tuple-element.92), channel_id=1, source_target_pairs={{0,1},{1,0},{2,3},{3,2},{4,5},{5,4},{6,7},{7,6},{8,9},{9,8},{10,11... | collective-permute-start | bytes 786440 | tf_op jit(solution)/shard_map/ppermute | solution.py:399
  200.0 1.2 collective-permute-done.30.refs_5_
  201.2 1.5 shard_map.75
  (41 shorter events, 9.6 us)
Async XLA Ops:
  4.0 27.5 %copy-start.1 = (s32[8]{0:T(128)S(1)}, s32[8]{0:T(128)}, u32[]{:S(2)}) copy-start(s32[8]{0:T(128)} %refs_1_.19) | copy-start | bytes 100
  4.0 27.5 %collective-permute-start.1 = (bf16[272,4096]{1,0:T(8,128)(2,1)S(1)}, bf16[272,4096]{1,0:T(8,128)(2,1)S(1)}, u32[]{:S(2)}, u32[]{:S(2)}) collective-permute-start(bf16[272,4096]{1,0:T(8,128)(2,1)S(1)} %shard_map.60), channel_id=1, source_target_pairs={{0,16},{1,49},{2,18},{3,51},{4,20},{5,53},{6,22},{7,55},{8,24},{9,... | collective-permute-start | bytes 6684680 | tf_op jit(solution)/shard_map/ppermute | solution.py:349
  7.8 46.2 %collective-permute-start = (bf16[256,4096]{1,0:T(8,128)(2,1)S(1)}, bf16[256,4096]{1,0:T(8,128)(2,1)S(1)}, u32[]{:S(2)}, u32[]{:S(2)}) collective-permute-start(bf16[256,4096]{1,0:T(8,128)(2,1)S(1)} %shard_map.59), channel_id=1, source_target_pairs={{0,16},{1,49},{2,18},{3,51},{4,20},{5,53},{6,22},{7,55},{8,24},{9,... | collective-permute-start | bytes 6291464 | tf_op jit(solution)/shard_map/ppermute | solution.py:349
  34.8 28.0 %collective-permute-start.2 = (s16[272,2048]{1,0:T(8,128)(2,1)S(1)}, s16[272,2048]{1,0:T(8,128)(2,1)S(1)}, u32[]{:S(2)}, u32[]{:S(2)}) collective-permute-start(s16[272,2048]{1,0:T(8,128)(2,1)S(1)} %get-tuple-element.48.refs_10_.refs_3_), channel_id=1, source_target_pairs={{0,8},{1,9},{2,10},{3,11},{4,12},{5,13},{6,14},{7,15},{8,72},{9,73... | collective-permute-start | bytes 3342344 | tf_op jit(solution)/shard_map/ppermute | solution.py:358
  36.6 26.2 %collective-permute-start.3 = (s16[272,2048]{1,0:T(8,128)(2,1)S(1)}, s16[272,2048]{1,0:T(8,128)(2,1)S(1)}, u32[]{:S(2)}, u32[]{:S(2)}) collective-permute-start(s16[272,2048]{1,0:T(8,128)(2,1)S(1)} %get-tuple-element.49.refs_11_.refs_4_), channel_id=1, source_target_pairs={{0,0},{1,1},{2,2},{3,3},{4,4},{5,5},{6,6},{7,7},{8,64},{9,65},{10,... | collective-permute-start | bytes 3342344 | tf_op jit(solution)/shard_map/ppermute | solution.py:358
  39.4 37.0 %collective-permute-start.7 = (bf16[256,4096]{1,0:T(8,128)(2,1)S(1)}, bf16[256,4096]{1,0:T(8,128)(2,1)S(1)}, u32[]{:S(2)}, u32[]{:S(2)}) collective-permute-start(bf16[256,4096]{1,0:T(8,128)(2,1)S(1)} %shard_map.65), channel_id=1, source_target_pairs={{0,16},{1,49},{2,18},{3,51},{4,20},{5,53},{6,22},{7,55},{8,24},{9,... | collective-permute-start | bytes 6291464 | tf_op jit(solution)/shard_map/ppermute | solution.py:349
  66.5 35.3 %collective-permute-start.4 = (bf16[256,4096]{1,0:T(8,128)(2,1)S(1)}, bf16[256,4096]{1,0:T(8,128)(2,1)S(1)}, u32[]{:S(2)}, u32[]{:S(2)}) collective-permute-start(bf16[256,4096]{1,0:T(8,128)(2,1)S(1)} %shard_map.64), channel_id=1, source_target_pairs={{0,16},{1,49},{2,18},{3,51},{4,20},{5,53},{6,22},{7,55},{8,24},{9,... | collective-permute-start | bytes 6291464 | tf_op jit(solution)/shard_map/ppermute | solution.py:349
  67.2 28.1 %collective-permute-start.5 = (s16[256,2048]{1,0:T(8,128)(2,1)S(1)}, s16[256,2048]{1,0:T(8,128)(2,1)S(1)}, u32[]{:S(2)}, u32[]{:S(2)}) collective-permute-start(s16[256,2048]{1,0:T(8,128)(2,1)S(1)} %get-tuple-element.54.refs_5_.refs_3_.refs_10_), channel_id=1, source_target_pairs={{0,8},{1,9},{2,10},{3,11},{4,12},{5,13},{6,14},{7,15},{8,72},{9,73... | collective-permute-start | bytes 3145736 | tf_op jit(solution)/shard_map/ppermute | solution.py:358
  71.2 24.1 %collective-permute-start.6 = (s16[256,2048]{1,0:T(8,128)(2,1)S(1)}, s16[256,2048]{1,0:T(8,128)(2,1)S(1)}, u32[]{:S(2)}, u32[]{:S(2)}) collective-permute-start(s16[256,2048]{1,0:T(8,128)(2,1)S(1)} %get-tuple-element.55.refs_6_.refs_4_.refs_11_), channel_id=1, source_target_pairs={{0,0},{1,1},{2,2},{3,3},{4,4},{5,5},{6,6},{7,7},{8,64},{9,65},{10,... | collective-permute-start | bytes 3145736 | tf_op jit(solution)/shard_map/ppermute | solution.py:358
  71.9 24.9 %collective-permute-start.8 = (s16[288,1024]{1,0:T(8,128)(2,1)S(1)}, s16[288,1024]{1,0:T(8,128)(2,1)S(1)}, u32[]{:S(2)}, u32[]{:S(2)}) collective-permute-start(s16[288,1024]{1,0:T(8,128)(2,1)S(1)} %get-tuple-element.52.refs_5_.refs_12_), channel_id=1, source_target_pairs={{0,0},{1,2},{2,1},{3,3},{4,4},{5,6},{6,5},{7,7},{8,8},{9,10},{10,9... | collective-permute-start | bytes 1769480 | tf_op jit(solution)/shard_map/ppermute | solution.py:364
  76.4 20.4 %collective-permute-start.9 = (s16[288,1024]{1,0:T(8,128)(2,1)S(1)}, s16[288,1024]{1,0:T(8,128)(2,1)S(1)}, u32[]{:S(2)}, u32[]{:S(2)}) collective-permute-start(s16[288,1024]{1,0:T(8,128)(2,1)S(1)} %get-tuple-element.53.refs_6_.refs_13_), channel_id=1, source_target_pairs={{0,4},{1,6},{2,5},{3,7},{4,0},{5,2},{6,1},{7,3},{8,12},{9,14},{10,... | collective-permute-start | bytes 1769480 | tf_op jit(solution)/shard_map/ppermute | solution.py:364
  96.9 14.9 %collective-permute-start.14 = (s16[272,1024]{1,0:T(8,128)(2,1)S(1)}, s16[272,1024]{1,0:T(8,128)(2,1)S(1)}, u32[]{:S(2)}, u32[]{:S(2)}) collective-permute-start(s16[272,1024]{1,0:T(8,128)(2,1)S(1)} %get-tuple-element.68.refs_10_), channel_id=1, source_target_pairs={{0,0},{1,2},{2,1},{3,3},{4,4},{5,6},{6,5},{7,7},{8,8},{9,10},{10,9... | collective-permute-start | bytes 1671176 | tf_op jit(solution)/shard_map/ppermute | solution.py:364
  97.6 28.0 %collective-permute-start.10 = (s16[256,2048]{1,0:T(8,128)(2,1)S(1)}, s16[256,2048]{1,0:T(8,128)(2,1)S(1)}, u32[]{:S(2)}, u32[]{:S(2)}) collective-permute-start(s16[256,2048]{1,0:T(8,128)(2,1)S(1)} %get-tuple-element.62.refs_5_), channel_id=1, source_target_pairs={{0,8},{1,9},{2,10},{3,11},{4,12},{5,13},{6,14},{7,15},{8,72},{9,73... | collective-permute-start | bytes 3145736 | tf_op jit(solution)/shard_map/ppermute | solution.py:358
  101.1 24.5 %collective-permute-start.11 = (s16[256,2048]{1,0:T(8,128)(2,1)S(1)}, s16[256,2048]{1,0:T(8,128)(2,1)S(1)}, u32[]{:S(2)}, u32[]{:S(2)}) collective-permute-start(s16[256,2048]{1,0:T(8,128)(2,1)S(1)} %get-tuple-element.63.refs_6_), channel_id=1, source_target_pairs={{0,0},{1,1},{2,2},{3,3},{4,4},{5,5},{6,6},{7,7},{8,64},{9,65},{10,... | collective-permute-start | bytes 3145736 | tf_op jit(solution)/shard_map/ppermute | solution.py:358
  105.1 19.7 %collective-permute-start.16 = (s16[288,1024]{1,0:T(8,128)(2,1)S(1)}, s16[288,1024]{1,0:T(8,128)(2,1)S(1)}, u32[]{:S(2)}, u32[]{:S(2)}) collective-permute-start(s16[288,1024]{1,0:T(8,128)(2,1)S(1)} %collective-permute-done.8.refs_12_), channel_id=1, source_target_pairs={{0,0},{1,16},{2,3},{3,19},{4,36},{5,52},{6,39},{7,55},{8,8},{9,24}... | collective-permute-start | bytes 1769480 | tf_op jit(solution)/shard_map/ppermute | solution.py:364
  105.8 19.0 %collective-permute-start.17 = (s16[288,1024]{1,0:T(8,128)(2,1)S(1)}, s16[288,1024]{1,0:T(8,128)(2,1)S(1)}, u32[]{:S(2)}, u32[]{:S(2)}) collective-permute-start(s16[288,1024]{1,0:T(8,128)(2,1)S(1)} %collective-permute-done.9.refs_13_), channel_id=1, source_target_pairs={{0,32},{1,48},{2,35},{3,51},{4,4},{5,20},{6,7},{7,23},{8,40},{9,56... | collective-permute-start | bytes 1769480 | tf_op jit(solution)/shard_map/ppermute | solution.py:364
  111.8 13.0 %collective-permute-start.15 = (s16[272,1024]{1,0:T(8,128)(2,1)S(1)}, s16[272,1024]{1,0:T(8,128)(2,1)S(1)}, u32[]{:S(2)}, u32[]{:S(2)}) collective-permute-start(s16[272,1024]{1,0:T(8,128)(2,1)S(1)} %get-tuple-element.69.refs_11_), channel_id=1, source_target_pairs={{0,4},{1,6},{2,5},{3,7},{4,0},{5,2},{6,1},{7,3},{8,12},{9,14},{10,... | collective-permute-start | bytes 1671176 | tf_op jit(solution)/shard_map/ppermute | solution.py:364
  124.9 12.5 %collective-permute-start.18 = (s16[272,1024]{1,0:T(8,128)(2,1)S(1)}, s16[272,1024]{1,0:T(8,128)(2,1)S(1)}, u32[]{:S(2)}, u32[]{:S(2)}) collective-permute-start(s16[272,1024]{1,0:T(8,128)(2,1)S(1)} %collective-permute-done.14), channel_id=1, source_target_pairs={{0,0},{1,16},{2,3},{3,19},{4,36},{5,52},{6,39},{7,55},{8,8},{9,24}... | collective-permute-start | bytes 1671176 | tf_op jit(solution)/shard_map/ppermute | solution.py:364
  127.1 22.1 %collective-permute-start.12 = (s16[256,2048]{1,0:T(8,128)(2,1)S(1)}, s16[256,2048]{1,0:T(8,128)(2,1)S(1)}, u32[]{:S(2)}, u32[]{:S(2)}) collective-permute-start(s16[256,2048]{1,0:T(8,128)(2,1)S(1)} %get-tuple-element.66.refs_5_), channel_id=1, source_target_pairs={{0,8},{1,9},{2,10},{3,11},{4,12},{5,13},{6,14},{7,15},{8,72},{9,73... | collective-permute-start | bytes 3145736 | tf_op jit(solution)/shard_map/ppermute | solution.py:358
  129.0 20.3 %collective-permute-start.13 = (s16[256,2048]{1,0:T(8,128)(2,1)S(1)}, s16[256,2048]{1,0:T(8,128)(2,1)S(1)}, u32[]{:S(2)}, u32[]{:S(2)}) collective-permute-start(s16[256,2048]{1,0:T(8,128)(2,1)S(1)} %get-tuple-element.67.refs_6_), channel_id=1, source_target_pairs={{0,0},{1,1},{2,2},{3,3},{4,4},{5,5},{6,6},{7,7},{8,64},{9,65},{10,... | collective-permute-start | bytes 3145736 | tf_op jit(solution)/shard_map/ppermute | solution.py:358
  129.7 16.4 %collective-permute-start.19 = (s16[272,1024]{1,0:T(8,128)(2,1)S(1)}, s16[272,1024]{1,0:T(8,128)(2,1)S(1)}, u32[]{:S(2)}, u32[]{:S(2)}) collective-permute-start(s16[272,1024]{1,0:T(8,128)(2,1)S(1)} %collective-permute-done.15), channel_id=1, source_target_pairs={{0,32},{1,48},{2,35},{3,51},{4,4},{5,20},{6,7},{7,23},{8,40},{9,56... | collective-permute-start | bytes 1671176 | tf_op jit(solution)/shard_map/ppermute | solution.py:364
  136.6 15.7 %collective-permute-start.20 = (s16[272,1024]{1,0:T(8,128)(2,1)S(1)}, s16[272,1024]{1,0:T(8,128)(2,1)S(1)}, u32[]{:S(2)}, u32[]{:S(2)}) collective-permute-start(s16[272,1024]{1,0:T(8,128)(2,1)S(1)} %get-tuple-element.82), channel_id=1, source_target_pairs={{0,0},{1,2},{2,1},{3,3},{4,4},{5,6},{6,5},{7,7},{8,8},{9,10},{10,9... | collective-permute-start | bytes 1671176 | tf_op jit(solution)/shard_map/ppermute | solution.py:364
  137.4 19.4 %collective-permute-start.21 = (s16[272,1024]{1,0:T(8,128)(2,1)S(1)}, s16[272,1024]{1,0:T(8,128)(2,1)S(1)}, u32[]{:S(2)}, u32[]{:S(2)}) collective-permute-start(s16[272,1024]{1,0:T(8,128)(2,1)S(1)} %get-tuple-element.83), channel_id=1, source_target_pairs={{0,4},{1,6},{2,5},{3,7},{4,0},{5,2},{6,1},{7,3},{8,12},{9,14},{10,... | collective-permute-start | bytes 1671176 | tf_op jit(solution)/shard_map/ppermute | solution.py:364
  149.2 1.6 copy-start
  156.8 12.1 %collective-permute-start.22 = (s16[272,1024]{1,0:T(8,128)(2,1)S(1)}, s16[272,1024]{1,0:T(8,128)(2,1)S(1)}, u32[]{:S(2)}, u32[]{:S(2)}) collective-permute-start(s16[272,1024]{1,0:T(8,128)(2,1)S(1)} %get-tuple-element.84), channel_id=1, source_target_pairs={{0,0},{1,2},{2,1},{3,3},{4,4},{5,6},{6,5},{7,7},{8,8},{9,10},{10,9... | collective-permute-start | bytes 1671176 | tf_op jit(solution)/shard_map/ppermute | solution.py:364
  157.5 15.1 %collective-permute-start.24 = (s16[272,1024]{1,0:T(8,128)(2,1)S(1)}, s16[272,1024]{1,0:T(8,128)(2,1)S(1)}, u32[]{:S(2)}, u32[]{:S(2)}) collective-permute-start(s16[272,1024]{1,0:T(8,128)(2,1)S(1)} %get-tuple-element.85), channel_id=1, source_target_pairs={{0,4},{1,6},{2,5},{3,7},{4,0},{5,2},{6,1},{7,3},{8,12},{9,14},{10,... | collective-permute-start | bytes 1671176 | tf_op jit(solution)/shard_map/ppermute | solution.py:364
  161.4 18.7 %collective-permute-start.26 = (s16[272,1024]{1,0:T(8,128)(2,1)S(1)}, s16[272,1024]{1,0:T(8,128)(2,1)S(1)}, u32[]{:S(2)}, u32[]{:S(2)}) collective-permute-start(s16[272,1024]{1,0:T(8,128)(2,1)S(1)} %collective-permute-done.20), channel_id=1, source_target_pairs={{0,0},{1,16},{2,3},{3,19},{4,36},{5,52},{6,39},{7,55},{8,8},{9,24}... | collective-permute-start | bytes 1671176 | tf_op jit(solution)/shard_map/ppermute | solution.py:364
  162.1 18.3 %collective-permute-start.27 = (s16[272,1024]{1,0:T(8,128)(2,1)S(1)}, s16[272,1024]{1,0:T(8,128)(2,1)S(1)}, u32[]{:S(2)}, u32[]{:S(2)}) collective-permute-start(s16[272,1024]{1,0:T(8,128)(2,1)S(1)} %collective-permute-done.21), channel_id=1, source_target_pairs={{0,32},{1,48},{2,35},{3,51},{4,4},{5,20},{6,7},{7,23},{8,40},{9,56... | collective-permute-start | bytes 1671176 | tf_op jit(solution)/shard_map/ppermute | solution.py:364
  168.9 19.5 %collective-permute-start.23 = (s16[272,1024]{1,0:T(8,128)(2,1)S(1)}, s16[272,1024]{1,0:T(8,128)(2,1)S(1)}, u32[]{:S(2)}, u32[]{:S(2)}) collective-permute-start(s16[272,1024]{1,0:T(8,128)(2,1)S(1)} %collective-permute-done.22), channel_id=1, source_target_pairs={{0,0},{1,16},{2,3},{3,19},{4,36},{5,52},{6,39},{7,55},{8,8},{9,24}... | collective-permute-start | bytes 1671176 | tf_op jit(solution)/shard_map/ppermute | solution.py:364
  172.6 21.0 %collective-permute-start.25 = (s16[272,1024]{1,0:T(8,128)(2,1)S(1)}, s16[272,1024]{1,0:T(8,128)(2,1)S(1)}, u32[]{:S(2)}, u32[]{:S(2)}) collective-permute-start(s16[272,1024]{1,0:T(8,128)(2,1)S(1)} %collective-permute-done.24), channel_id=1, source_target_pairs={{0,32},{1,48},{2,35},{3,51},{4,4},{5,20},{6,7},{7,23},{8,40},{9,56... | collective-permute-start | bytes 1671176 | tf_op jit(solution)/shard_map/ppermute | solution.py:364
  182.4 18.8 %collective-permute-start.28 = (bf16[768,512]{1,0:T(8,128)(2,1)S(1)}, bf16[768,512]{1,0:T(8,128)(2,1)S(1)}, u32[]{:S(2)}, u32[]{:S(2)}) collective-permute-start(bf16[768,512]{1,0:T(8,128)(2,1)S(1)} %get-tuple-element.91), channel_id=1, source_target_pairs={{0,1},{1,0},{2,3},{3,2},{4,5},{5,4},{6,7},{7,6},{8,9},{9,8},{10,11... | collective-permute-start | bytes 2359304 | tf_op jit(solution)/shard_map/ppermute | solution.py:397
  195.5 5.7 %collective-permute-start.29 = (bf16[256,512]{1,0:T(8,128)(2,1)S(1)}, bf16[256,512]{1,0:T(8,128)(2,1)S(1)}, u32[]{:S(2)}, u32[]{:S(2)}) collective-permute-start(bf16[256,512]{1,0:T(8,128)(2,1)S(1)} %get-tuple-element.92), channel_id=1, source_target_pairs={{0,1},{1,0},{2,3},{3,2},{4,5},{5,4},{6,7},{7,6},{8,9},{9,8},{10,11... | collective-permute-start | bytes 786440 | tf_op jit(solution)/shard_map/ppermute | solution.py:399
  200.0 1.2 collective-permute-start.30
